TPU v7x, 32 devices: a whole 2x2x4 slice. The times are simulated.
32 devices in a mesh: dp: 16 (over z, y, x), seq: 2 (over core).
Axes of the slice: x: 2, y: 2, z: 4, core: 2. Of those that a mesh axis runs over, the one named last changes fastest.
Arguments:
- tokens: bfloat16 [16384, 768], P(('dp', 'seq')), may hold values from -6 to 6
- skip_values: bfloat16 [16384, 384], P(('dp', 'seq')), may hold values from -6 to 6
- doc_lengths: int32 [16, 6], P('dp'), may hold values from 1 to 682, as said below
- gain_first: bfloat16 [768], replicated, may hold values from 0.099609375 to 1.8984375
- shift_first: bfloat16 [768], replicated, may hold values from -3 to 3
- query_weight: bfloat16 [768, 768], replicated, may hold values from -0.21875 to 0.21875
- query_bias: bfloat16 [768], replicated, may hold values from -3 to 3
- key_weight: bfloat16 [768, 768], replicated, may hold values from -0.21875 to 0.21875
- value_weight: bfloat16 [768, 384], replicated, may hold values from -0.21875 to 0.21875
- value_bias: bfloat16 [384], replicated, may hold values from -3 to 3
- out_weight: bfloat16 [768, 768], replicated, may hold values from -0.875 to 0.875
- out_bias: bfloat16 [768], replicated, may hold values from -3 to 3
- gain_second: bfloat16 [768], replicated, may hold values from 0.099609375 to 1.8984375
- shift_second: bfloat16 [768], replicated, may hold values from -3 to 3
- up_weight: bfloat16 [768, 3072], replicated, may hold values from -0.21875 to 0.21875
- up_bias: bfloat16 [3072], replicated, may hold values from -3 to 3
- down_weight: bfloat16 [3072, 768], replicated, may hold values from -0.109375 to 0.109375
- down_bias: bfloat16 [768], replicated, may hold values from -3 to 3
- cotangent: bfloat16 [16384, 768], P(('dp', 'seq')), may hold values from -6 to 6
Outputs:
- output: bfloat16 [16384, 768], P(('dp', 'seq'))
- grad_tokens: bfloat16 [16384, 768], P(('dp', 'seq'))
- grad_skip_values: bfloat16 [16384, 384], P(('dp', 'seq'))
- grad_gain_first: float32 [768], replicated
- grad_shift_first: float32 [768], replicated
- grad_query_weight: float32 [768, 768], P('dp')
- grad_query_bias: float32 [768], replicated
- grad_key_weight: float32 [768, 768], P('dp')
- grad_value_weight: float32 [768, 384], P('dp')
- grad_value_bias: float32 [384], replicated
- grad_out_weight: float32 [768, 768], P('dp')
- grad_out_bias: float32 [768], replicated
- grad_gain_second: float32 [768], replicated
- grad_shift_second: float32 [768], replicated
- grad_up_weight: float32 [768, 3072], P('dp')
- grad_up_bias: float32 [3072], replicated
- grad_down_weight: float32 [3072, 768], P('dp')
- grad_down_bias: float32 [768], replicated
Inputs may be any that keep to these rules, and one draw needn't show every extreme that they name: `doc_lengths`: each row lists 6 - 1 document lengths in order, then the number of padding positions at the row's end (1 or more); a row's entries sum to 1024, and exactly one document of each row has 682 positions.
All inputs are finite; a program needn't handle non-finite values.
Results may differ from a plain program's by a relative error of at most 0.014.
Values may be sent and summed in bfloat16 or wider, within the bound.
No kernel may reach another device: no remote copies, remote signals or barrier semaphores. Data moves between devices by JAX's collectives and lax.ppermute only.
A program may use at most 192 MiB of HBM per device.

v0:
```python
import jax
import jax.numpy as jnp
from jax import lax
from jax.sharding import PartitionSpec as P

HEAD = 64
FRESH = 6


def layer_norm(values, gain, shift):
    centre = values - jnp.mean(values, axis=-1, keepdims=True)
    spread = jnp.mean(centre * centre, axis=-1, keepdims=True)
    return centre * lax.rsqrt(spread + 1e-05) * gain + shift


def gelu_tanh(values):
    return jax.nn.gelu(values, approximate=True)


def allowed_pairs(length_row, total):
    count = length_row.shape[0]
    bounds = jnp.cumsum(length_row)
    places = jnp.arange(total, dtype=jnp.int32)
    segment = jnp.sum((places[:, None] >= bounds[None, : count - 1]).astype(jnp.int32), axis=1)
    matching = segment[:, None] == segment[None, :]
    causal = places[None, :] <= places[:, None]
    usable = (segment[None, :] != count - 1) | (places[None, :] == places[:, None])
    return matching & causal & usable


def side_by_side(stacked):
    heads_here, length, width = stacked.shape
    return jnp.transpose(stacked, (1, 0, 2)).reshape(length, heads_here * width)


def per_device(
    tokens,
    skip_values,
    doc_lengths,
    gain_first,
    shift_first,
    query_weight,
    query_bias,
    key_weight,
    value_weight,
    value_bias,
    out_weight,
    out_bias,
    gain_second,
    shift_second,
    up_weight,
    up_bias,
    down_weight,
    down_bias,
    cotangent,
):
    f32 = jnp.float32
    bf16 = jnp.bfloat16
    groups = lax.axis_size("seq")
    row_length = tokens.shape[0] * groups
    score_scale = HEAD ** (-0.5)
    fresh_width = FRESH * HEAD
    inputs = tokens.astype(f32)
    normed_first, norm_back_first = jax.vjp(
        layer_norm, inputs, gain_first.astype(f32), shift_first.astype(f32)
    )
    normed_low = normed_first.astype(bf16)
    queries = (jnp.dot(normed_low, query_weight, preferred_element_type=f32) + query_bias).astype(
        bf16
    )
    keys_low = jnp.dot(normed_low, key_weight, preferred_element_type=f32).astype(bf16)
    fresh = (jnp.dot(normed_low, value_weight, preferred_element_type=f32) + value_bias).astype(
        bf16
    )
    values_all = jnp.concatenate([fresh, skip_values], axis=1)
    head_query, head_key, head_value = (
        lax.all_to_all(queries, "seq", split_axis=1, concat_axis=0, tiled=True),
        lax.all_to_all(keys_low, "seq", split_axis=1, concat_axis=0, tiled=True),
        lax.all_to_all(values_all, "seq", split_axis=1, concat_axis=0, tiled=True),
    )
    allowed = allowed_pairs(doc_lengths[0], row_length)
    heads_here = head_query.shape[1] // HEAD
    head_list = jnp.arange(heads_here, dtype=jnp.int32)

    def head_scores(query_part, key_part):
        raw = (
            jnp.einsum("qd,kd->qk", query_part, key_part, preferred_element_type=f32) * score_scale
        )
        return jnp.where(allowed, raw, -1e30)

    def attend(head_index):
        column = head_index * HEAD
        query_part = lax.dynamic_slice_in_dim(head_query, column, HEAD, 1)
        key_part = lax.dynamic_slice_in_dim(head_key, column, HEAD, 1)
        value_part = lax.dynamic_slice_in_dim(head_value, column, HEAD, 1)
        masked = head_scores(query_part, key_part)
        row_peak = jnp.max(masked, axis=1, keepdims=True)
        log_total = row_peak + jnp.log(jnp.sum(jnp.exp(masked - row_peak), axis=1, keepdims=True))
        attention = jnp.exp(masked - log_total).astype(bf16)
        result = jnp.dot(attention, value_part, preferred_element_type=f32)
        return (result.astype(bf16), log_total[:, 0])

    head_outputs, log_totals = lax.map(attend, head_list)
    attended = lax.all_to_all(
        side_by_side(head_outputs), "seq", split_axis=0, concat_axis=1, tiled=True
    )
    middle = inputs + jnp.dot(attended, out_weight, preferred_element_type=f32) + out_bias
    normed_second, norm_back_second = jax.vjp(
        layer_norm, middle, gain_second.astype(f32), shift_second.astype(f32)
    )
    second_low = normed_second.astype(bf16)
    hidden_pre = jnp.dot(second_low, up_weight, preferred_element_type=f32) + up_bias
    activated, gelu_back = jax.vjp(gelu_tanh, hidden_pre)
    activated_low = activated.astype(bf16)
    result_all = (
        middle + jnp.dot(activated_low, down_weight, preferred_element_type=f32) + down_bias
    )
    output = result_all.astype(bf16)
    grad_output = cotangent.astype(f32)
    grad_down_weight = jnp.einsum("tf,td->fd", activated_low, cotangent, preferred_element_type=f32)
    grad_down_bias = jnp.sum(grad_output, axis=0)
    grad_activated = jnp.einsum("td,fd->tf", cotangent, down_weight, preferred_element_type=f32)
    grad_hidden = gelu_back(grad_activated)[0].astype(bf16)
    grad_up_bias = jnp.sum(grad_hidden.astype(f32), axis=0)
    grad_up_weight = jnp.einsum("td,tf->df", second_low, grad_hidden, preferred_element_type=f32)
    grad_normed_second = jnp.einsum("tf,df->td", grad_hidden, up_weight, preferred_element_type=f32)
    grad_middle_norm, grad_gain_second, grad_shift_second = norm_back_second(grad_normed_second)
    grad_middle = grad_output + grad_middle_norm
    grad_branch = grad_middle.astype(bf16)
    grad_out_bias = jnp.sum(grad_branch.astype(f32), axis=0)
    grad_out_weight = jnp.einsum("td,te->de", attended, grad_branch, preferred_element_type=f32)
    grad_attended = jnp.einsum(
        "te,de->td", grad_branch, out_weight, preferred_element_type=f32
    ).astype(bf16)
    grad_heads = lax.all_to_all(grad_attended, "seq", split_axis=1, concat_axis=0, tiled=True)

    def differentiate(head_index):
        column = head_index * HEAD
        query_part = lax.dynamic_slice_in_dim(head_query, column, HEAD, 1)
        key_part = lax.dynamic_slice_in_dim(head_key, column, HEAD, 1)
        value_part = lax.dynamic_slice_in_dim(head_value, column, HEAD, 1)
        grad_part = lax.dynamic_slice_in_dim(grad_heads, column, HEAD, 1)
        masked = head_scores(query_part, key_part)
        attention = jnp.exp(masked - log_totals[head_index][:, None])
        attention_low = attention.astype(bf16)
        grad_probs = jnp.einsum("qd,kd->qk", grad_part, value_part, preferred_element_type=f32)
        grad_value = jnp.einsum("qk,qd->kd", attention_low, grad_part, preferred_element_type=f32)
        row_term = jnp.sum(attention * grad_probs, axis=1, keepdims=True)
        grad_scores = (attention * (grad_probs - row_term)).astype(bf16)
        grad_query = jnp.dot(grad_scores, key_part, preferred_element_type=f32) * score_scale
        grad_key = (
            jnp.einsum("qk,qd->kd", grad_scores, query_part, preferred_element_type=f32)
            * score_scale
        )
        return (grad_query.astype(bf16), grad_key.astype(bf16), grad_value.astype(bf16))

    grad_query_heads, grad_key_heads, grad_value_heads = lax.map(differentiate, head_list)
    back_query, back_key, back_value = (
        lax.all_to_all(
            side_by_side(grad_query_heads), "seq", split_axis=0, concat_axis=1, tiled=True
        ),
        lax.all_to_all(
            side_by_side(grad_key_heads), "seq", split_axis=0, concat_axis=1, tiled=True
        ),
        lax.all_to_all(
            side_by_side(grad_value_heads), "seq", split_axis=0, concat_axis=1, tiled=True
        ),
    )
    grad_skip_values = back_value[:, fresh_width:]
    grad_fresh = back_value[:, :fresh_width]
    grad_query_weight = jnp.einsum("td,te->de", normed_low, back_query, preferred_element_type=f32)
    grad_key_weight = jnp.einsum("td,te->de", normed_low, back_key, preferred_element_type=f32)
    grad_value_weight = jnp.einsum("td,te->de", normed_low, grad_fresh, preferred_element_type=f32)
    grad_query_bias = jnp.sum(back_query.astype(f32), axis=0)
    grad_value_bias = jnp.sum(grad_fresh.astype(f32), axis=0)
    grad_normed = (
        jnp.einsum("te,de->td", back_query, query_weight, preferred_element_type=f32)
        + jnp.einsum("te,de->td", back_key, key_weight, preferred_element_type=f32)
        + jnp.einsum("te,de->td", grad_fresh, value_weight, preferred_element_type=f32)
    )
    grad_input_norm, grad_gain_first, grad_shift_first = norm_back_first(grad_normed)
    grad_tokens = (grad_middle + grad_input_norm).astype(bf16)
    matrices = (
        grad_query_weight,
        grad_key_weight,
        grad_value_weight,
        grad_out_weight,
        grad_up_weight,
        grad_down_weight,
    )
    shares = (
        lax.psum_scatter(matrices[0], "dp", scatter_dimension=0, tiled=True),
        lax.psum_scatter(matrices[1], "dp", scatter_dimension=0, tiled=True),
        lax.psum_scatter(matrices[2], "dp", scatter_dimension=0, tiled=True),
        lax.psum_scatter(matrices[3], "dp", scatter_dimension=0, tiled=True),
        lax.psum_scatter(matrices[4], "dp", scatter_dimension=0, tiled=True),
        lax.psum_scatter(matrices[5], "dp", scatter_dimension=0, tiled=True),
    )
    summed = (
        lax.psum(shares[0].astype(jnp.bfloat16), "seq").astype(jnp.float32),
        lax.psum(shares[1].astype(jnp.bfloat16), "seq").astype(jnp.float32),
        lax.psum(shares[2].astype(jnp.bfloat16), "seq").astype(jnp.float32),
        lax.psum(shares[3].astype(jnp.bfloat16), "seq").astype(jnp.float32),
        lax.psum(shares[4].astype(jnp.bfloat16), "seq").astype(jnp.float32),
        lax.psum(shares[5].astype(jnp.bfloat16), "seq").astype(jnp.float32),
    )
    vectors = lax.psum(
        (
            grad_gain_first,
            grad_shift_first,
            grad_query_bias,
            grad_value_bias,
            grad_out_bias,
            grad_gain_second,
            grad_shift_second,
            grad_up_bias,
            grad_down_bias,
        ),
        ("dp", "seq"),
    )
    return (
        output,
        grad_tokens,
        grad_skip_values,
        vectors[0],
        vectors[1],
        summed[0],
        vectors[2],
        summed[1],
        summed[2],
        vectors[3],
        summed[3],
        vectors[4],
        vectors[5],
        vectors[6],
        summed[4],
        vectors[7],
        summed[5],
        vectors[8],
    )


def solution(mesh):
    return jax.shard_map(
        per_device,
        mesh=mesh,
        in_specs=(
            P(("dp", "seq"), None),
            P(("dp", "seq"), None),
            P("dp", None),
            P(),
            P(),
            P(),
            P(),
            P(),
            P(),
            P(),
            P(),
            P(),
            P(),
            P(),
            P(),
            P(),
            P(),
            P(),
            P(("dp", "seq"), None),
        ),
        out_specs=(
            P(("dp", "seq"), None),
            P(("dp", "seq"), None),
            P(("dp", "seq"), None),
            P(),
            P(),
            P("dp", None),
            P(),
            P("dp", None),
            P("dp", None),
            P(),
            P("dp", None),
            P(),
            P(),
            P(),
            P("dp", None),
            P(),
            P("dp", None),
            P(),
        ),
        check_vma=False,
    )
```

profile of v0, /device:TPU:0, one launch (start us, length us, event | category | flops | bytes accessed | tf_op | source)
XLA Modules:
  0.0 1043.3 jit_solution(4700252212194257103)
XLA Ops:
  30.5 6.3 all_to_all.152
  38.3 53.8 %while.28 = (s32[]{:T(128)}, bf16[6,1024,64]{1,2,0:T(8,128)(2,1)}, f32[6,1024]{1,0:T(8,128)}, s32[6]{0:T(128)}, bf16[1024,384]{1,0:T(8,128)(2,1)S(1)}, /*index=5...) while((s32[]{:T(128)}, bf16[6,1024,64]{1,2,0:T(8,128)(2,1)}, ...), condition=%wide.region_7.8_spmd.clone, body=%wide.region_4.7_spmd.clone.sunk | while | flops 282131456 | bytes 13548223 | solution.py:103
  97.5 4.3 all-to-all-start.3
  107.4 5.2 fusion.78
  112.6 7.2 convert_reduce_fusion
  140.8 103.3 %while.29 = (s32[]{:T(128)}, bf16[6,1024,64]{1,2,0:T(8,128)(2,1)}, bf16[6,1024,64]{1,2,0:T(8,128)(2,1)}, bf16[6,1024,64]{1,2,0:T(8,128)(2,1)}, s32[6]{0:T(128)S(...) while((s32[]{:T(128)}, bf16[6,1024,64]{1,2,0:T(8,128)(2,1)}, ...), condition=%wide.region_14.15_spmd.clone, body=%wide.region_12.14_spmd.clone.sunk | while | flops 687143936 | bytes 50496292 | solution.py:157
  147.5 4.2 multiply_reduce_fusion.5
  164.8 4.1 multiply_reduce_fusion.5
  182.0 4.2 multiply_reduce_fusion.5
  199.2 4.1 multiply_reduce_fusion.5
  233.6 4.1 multiply_reduce_fusion.5
  246.7 4.4 all_to_all.153
  255.5 4.4 all_to_all.154
  263.7 7.2 fusion.77
  272.1 10.3 fusion.79
  286.8 6.3 all_to_all.155
  308.8 43.5 %all-reduce = (f32[768]{0:T(1024)}, f32[768]{0:T(1024)}, f32[768]{0:T(1024)}, f32[384]{0:T(512)}, f32[768]{0:T(1024)}, /*index=5*/f32[768]{0:T(1024)}, f32[768]{0:T(1024)}, f32[3072]{0:T(1024)}, f32[768]{0:T(1024)}) all-reduce(f32[768]{0:T(1024)S(1)} %get-tuple-element.213, ...), channel_id=1, replica_groups=mesh['dp'=16,'seq'=2] {'dp','seq'}, use_global_device_ids=true, to_apply=%region_18.19 | all-reduce | flops 8832 | bytes 70656 | tf_op jit(solution)/shard_map/psum | solution.py:207
  353.9 40.2 %reduce-scatter.7.cloned.1.call-done = f32[48,768]{1,0:T(8,128)} async-done(((f32[768,768]{1,0:T(8,128)}), f32[48,768]{1,0:T(8,128)}) %reduce-scatter.7.cloned.1.call-update) | async-done | bytes 147472 | tf_op jit(solution)/shard_map/reduce_scatter | solution.py:192
  395.6 131.1 %reduce-scatter.9.cloned.1.call-done = f32[48,768]{1,0:T(8,128)} async-done(((f32[768,768]{1,0:T(8,128)}), f32[48,768]{1,0:T(8,128)}) %reduce-scatter.9.cloned.1.call-update) | async-done | bytes 147472 | tf_op jit(solution)/shard_map/reduce_scatter | solution.py:193
  528.2 175.2 %reduce-scatter.15.cloned.1.call-done = f32[48,3072]{1,0:T(8,128)} async-done(((f32[768,3072]{1,0:T(8,128)}), f32[48,3072]{1,0:T(8,128)}) %reduce-scatter.15.cloned.1.call-update) | async-done | bytes 589840 | tf_op jit(solution)/shard_map/reduce_scatter | solution.py:196
  705.2 173.7 %reduce-scatter.17.cloned.1.call-done = f32[192,768]{1,0:T(8,128)} async-done(((f32[3072,768]{1,0:T(8,128)}), f32[192,768]{1,0:T(8,128)}) %reduce-scatter.17.cloned.1.call-update) | async-done | bytes 589840 | tf_op jit(solution)/shard_map/reduce_scatter | solution.py:197
  880.7 9.1 add_convert_fusion.1
  889.8 117.7 %reduce-scatter.11.cloned.1.call-done = f32[48,384]{1,0:T(8,128)} async-done(((f32[768,384]{1,0:T(8,128)}), f32[48,384]{1,0:T(8,128)}) %reduce-scatter.11.cloned.1.call-update) | async-done | bytes 73744 | tf_op jit(solution)/shard_map/reduce_scatter | solution.py:194
  1012.5 18.0 %all-reduce.4.cloned.1.call-done = (bf16[48,768]{1,0:T(8,128)(2,1)}, bf16[48,768]{1,0:T(8,128)(2,1)}, bf16[48,768]{1,0:T(8,128)(2,1)}, bf16[48,3072]{1,0:T(8,128)(2,1)}, bf16[192,768]{1,0:T(8,128)(2,1)}) async-done(((bf16[48,768]{1,0:T(8,128)(2,1)}, bf16[48,768]{1,0:T(8,128)(2,1)}, bf16[48,768]{1,0:T(8,128)(2,1)}, bf16[48,3072]{1,0:T(8,128)(2,1)}, bf16[192,768]{1,0:T(8,128)(2,1)}), ...) | async-done | bytes 811024 | tf_op jit(solution)/shard_map/psum | solution.py:200
  (316 shorter events, 223.7 us)
Async XLA Ops:
  7.2 96.7 %copy-start = (bf16[768,768]{1,0:T(8,128)(2,1)S(1)}, bf16[768,768]{1,0:T(8,128)(2,1)}, u32[]{:S(2)}) copy-start(bf16[768,768]{1,0:T(8,128)(2,1)} %param.33) | copy-start | bytes 3538948
  10.3 13.7 %copy-start.40 = (f32[768]{0:T(1024)}, f32[768]{0:T(1024)S(1)}, u32[]{:S(2)}) copy-start(f32[768]{0:T(1024)S(1)} %convert_element_type.141) | copy-start | bytes 9220
  12.2 6.7 all-to-all-start.2
  19.0 11.5 %all-to-all-start = ((bf16[512,2,384]{2,0,1:T(8,128)(2,1)}), bf16[512,2,384]{2,0,1:T(8,128)(2,1)S(1)}, u32[]{:S(2)}, u32[]{:S(2)}) async-start(bf16[512,2,384]{2,0,1:T(8,128)(2,1)} %bitcast.97), calls=%async_computation | async-start | bytes 1572864 | tf_op jit(solution)/shard_map/all_to_all | solution.py:77
  97.5 6.4 all-to-all-start.3
  101.8 250.5 %reduce-scatter.13.cloned.1.call-start = ((), (), s32[]{:S(2)}) async-start(), calls=%async_computation.17 | async-start | bytes 2506752 | tf_op jit(solution)/shard_map/reduce_scatter | solution.py:195
  105.9 17.4 %copy-start.6 = (f32[512,768]{1,0:T(8,128)}, f32[512,768]{1,0:T(8,128)S(1)}, u32[]{:S(2)}) copy-start(f32[512,768]{1,0:T(8,128)S(1)} %get-tuple-element.287) | copy-start | bytes 4718596
  106.0 17.4 %copy-start.25 = (f32[512]{0:T(512)}, f32[512]{0:T(512)S(1)}, u32[]{:S(2)}) copy-start(f32[512]{0:T(512)S(1)} %broadcast_multiply_fusion) | copy-start | bytes 6148
  106.0 6.6 slice-start.2
  106.6 16.8 %copy-start.37 = (f32[512]{0:T(512)}, f32[512]{0:T(512)S(1)}, u32[]{:S(2)}) copy-start(f32[512]{0:T(512)S(1)} %fusion.75) | copy-start | bytes 6148
  106.7 16.7 %copy-start.31 = (f32[768]{0:T(1024)}, f32[768]{0:T(1024)S(1)}, u32[]{:S(2)}) copy-start(f32[768]{0:T(1024)S(1)} %convert_element_type.150) | copy-start | bytes 9220
  107.3 12.5 %slice-start = ((s8[4718592]{0:T(1024)(128)(4,1)}), s8[4194304]{0:T(1024)(128)(4,1)S(1)}, s32[]{:S(2)}) async-start(s8[4718592]{0:T(1024)(128)(4,1)} %bitcast.141), calls=%async_computation.21 | async-start | bytes 8388608
  112.6 7.2 copy-start.55
  112.6 7.2 slice-start.1
  132.4 5.5 all-to-all-start.4
  136.0 258.1 %reduce-scatter.7.cloned.1.call-start = ((), (), s32[]{:S(2)}) async-start(), calls=%async_computation.14 | async-start | bytes 2506752 | tf_op jit(solution)/shard_map/reduce_scatter | solution.py:192
  253.7 272.9 %reduce-scatter.9.cloned.1.call-start = ((), (), s32[]{:S(2)}) async-start(), calls=%async_computation.15 | async-start | bytes 2506752 | tf_op jit(solution)/shard_map/reduce_scatter | solution.py:193
  262.4 441.0 %reduce-scatter.15.cloned.1.call-start = ((), (), s32[]{:S(2)}) async-start(), calls=%async_computation.18 | async-start | bytes 10027008 | tf_op jit(solution)/shard_map/reduce_scatter | solution.py:196
  271.0 607.9 %reduce-scatter.17.cloned.1.call-start = ((), (), s32[]{:S(2)}) async-start(), calls=%async_computation.19 | async-start | bytes 10027008 | tf_op jit(solution)/shard_map/reduce_scatter | solution.py:197
  282.4 725.1 %reduce-scatter.11.cloned.1.call-start = ((), (), s32[]{:S(2)}) async-start(), calls=%async_computation.16 | async-start | bytes 1253376 | tf_op jit(solution)/shard_map/reduce_scatter | solution.py:194
  296.5 734.0 %all-reduce.4.cloned.1.call-start = ((), (), s32[]{:S(2)}) async-start(), calls=%async_computation.20 | async-start | bytes 1622016 | tf_op jit(solution)/shard_map/psum | solution.py:200
  352.3 528.4 %copy-start.35 = (f32[3072]{0:T(1024)S(1)}, f32[3072]{0:T(1024)}, u32[]{:S(2)}) copy-start(f32[3072]{0:T(1024)} %copy-done.33) | copy-start | bytes 36868
  352.3 528.4 %copy-start.44 = (f32[768]{0:T(1024)S(1)}, f32[768]{0:T(1024)}, u32[]{:S(2)}) copy-start(f32[768]{0:T(1024)} %convert_element_type.155) | copy-start | bytes 9220
  880.7 155.5 %copy-start.1 = (bf16[768,768]{1,0:T(8,128)(2,1)S(1)}, bf16[768,768]{1,0:T(8,128)(2,1)}, u32[]{:S(2)}) copy-start(bf16[768,768]{1,0:T(8,128)(2,1)} %param.33) | copy-start | bytes 3538948
  (53 other events, 132.4 us)
Sparse Core Ops, SparseCore 0:
  129.6 131.1 reduce-scatter.12
  266.5 127.5 reduce-scatter.6
  398.9 127.6 reduce-scatter.8
  533.1 170.2 reduce-scatter.14
  708.9 169.8 reduce-scatter.16
  884.2 123.2 reduce-scatter.10
  1012.1 18.3 all-reduce.3
where the time goes:
time: 1050 us; the launch traced here: 1040 us
  waiting for transfers between devices  658 us (63%)
  matrix products  169 us (16%)
  blocking collectives  68.3 us (7%)
  local copies, waits for them, and re-layouts  55.9 us (5%)
  other arithmetic  40.6 us (4%)
  loops' own time  19.7 us (2%)
  starting transfers between devices  16 us (2%)
  between operations  15.2 us (1%)
    reduce_scatter x1, waiting for transfers between devices, per_device(): lax.psum_scatter(matrices[4], 'dp', scatter_dimension=0, tiled=True)  175 us
    reduce_scatter x1, waiting for transfers between devices, per_device(): lax.psum_scatter(matrices[5], 'dp', scatter_dimension=0, tiled=True)  174 us
    reduce_scatter x1, waiting for transfers between devices, per_device(): lax.psum_scatter(matrices[1], 'dp', scatter_dimension=0, tiled=True)  131 us
    reduce_scatter x1, waiting for transfers between devices, per_device(): lax.psum_scatter(matrices[2], 'dp', scatter_dimension=0, tiled=True)  118 us
    dot_general x12, matrix products, head_scores(): jnp.einsum('qd,kd->qk', query_part, key_part, preferred_element_type=f32)  46.2 us
    psum x1, blocking collectives, per_device(): lax.psum((grad_gain_first, grad_shift_first, grad_query_bias, grad_value_...  43.5 us
    reduce_scatter x1, waiting for transfers between devices, per_device(): lax.psum_scatter(matrices[0], 'dp', scatter_dimension=0, tiled=True)  40.2 us
  transfers between devices with their start and end apart: 11, of which 8 were waited for; matrix products, arithmetic and copies ran while one was open for 16% of the time, Pallas kernels for 0%

commit v1 on v0

v1 whole, which is shorter than its diff:
```python
import functools

import jax
import jax.numpy as jnp
from jax import lax
from jax.experimental import pallas as pl
from jax.experimental.pallas import tpu as pltpu
from jax.sharding import PartitionSpec as P

HEAD = 64
FRESH = 6
PAIR = 2 * HEAD
QB = 256
LOG2E = 1.4426950408889634
GELU_C = 0.7978845608028654
GELU_A = 0.044715
f32 = jnp.float32
bf16 = jnp.bfloat16
NT = (((1,), (1,)), ((), ()))
TN = (((0,), (0,)), ((), ()))
CORE, PLACE, BOUND, PLACE_OTH = 0, 1, 17, 22
V_UP, V_DOWN, V_OUT, V_GAIN2, V_SHIFT2, V_GAIN1, V_SHIFT1, V_QUERY, V_VALUE = 0, 8, 10, 12, 14, 16, 18, 20, 22
V_ROWS = 24


def dot(left, right):
    return jnp.dot(left, right, preferred_element_type=f32)


def dot_nt(left, right):
    return lax.dot_general(left, right, NT, preferred_element_type=f32)


def dot_tn(left, right):
    return lax.dot_general(left, right, TN, preferred_element_type=f32)


def row_of(ref):
    return ref[...].astype(f32).reshape(1, -1)


def normalise(values):
    centre = values - jnp.mean(values, axis=-1, keepdims=True)
    spread = jnp.mean(centre * centre, axis=-1, keepdims=True)
    scale = lax.rsqrt(spread + 1e-05)
    return centre * scale, scale


def params(limit_mb, axes):
    return pltpu.CompilerParams(vmem_limit_bytes=limit_mb << 20, dimension_semantics=("arbitrary",) * axes)


def whole(shape):
    return pl.BlockSpec(shape, lambda *_: (0,) * len(shape))


def sds(shape, dtype):
    return jax.ShapeDtypeStruct(shape, dtype)


def project_kernel(scal, own, oth, skip_own, skip_oth, gain, shift, wq, bq, wk, wv, bv, q_ref, k_ref, v_ref, n_ref):
    step = pl.program_id(0)
    core = scal[CORE]
    mine = step < 2
    tokens = jnp.where(mine, own[...], oth[...]).astype(f32)
    xhat, _ = normalise(tokens)
    normed = (xhat * row_of(gain) + row_of(shift)).astype(bf16)
    n_ref[0] = normed
    q_ref[0] = (dot(normed, wq[...]) + row_of(bq)).astype(bf16) * jnp.asarray(HEAD**-0.5, bf16)
    k_ref[0] = dot(normed, wk[...]).astype(bf16)

    @pl.when(core == 0)
    def _():
        v_ref[0] = (dot(normed, wv[...]) + row_of(bv)).astype(bf16)

    @pl.when(core != 0)
    def _():
        v_ref[0] = jnp.where(mine, skip_own[...], skip_oth[...])


def project(scal, own, oth, skip_own, skip_oth, gain, shift, wq, bq, wk, wv, bv):
    rows, width = own.shape
    half = width // 2
    tile = rows // 2
    first = lambda s, sc: (jnp.minimum(s, 1), 0)
    second = lambda s, sc: (jnp.maximum(s - 2, 0), 0)
    col = lambda s, sc: (0, sc[CORE])
    out = lambda s, sc: (s // 2, s % 2, 0)
    return pl.pallas_call(
        project_kernel,
        grid_spec=pltpu.PrefetchScalarGridSpec(
            num_scalar_prefetch=1,
            grid=(4,),
            in_specs=[
                pl.BlockSpec((tile, width), first),
                pl.BlockSpec((tile, width), second),
                pl.BlockSpec((tile, half), first),
                pl.BlockSpec((tile, half), second),
                whole((width,)),
                whole((width,)),
                pl.BlockSpec((width, half), col),
                pl.BlockSpec((1, half), col),
                pl.BlockSpec((width, half), col),
                whole((width, half)),
                whole((half,)),
            ],
            out_specs=[pl.BlockSpec((1, tile, half), out)] * 3 + [pl.BlockSpec((1, tile, width), out)],
        ),
        out_shape=[sds((2, rows, half), bf16)] * 3 + [sds((2, rows, width), bf16)],
        compiler_params=params(40, 1),
    )(scal, own, oth, skip_own, skip_oth, gain, shift, wq, bq.reshape(1, -1), wk, wv, bv)


def first_allowed(scal, total):
    place = lax.broadcasted_iota(jnp.int32, (1, total), 1)
    start = jnp.zeros((1, total), jnp.int32)
    for k in range(4):
        start = jnp.where(place >= scal[BOUND + k], scal[BOUND + k], start)
    return jnp.where(place >= scal[BOUND + 4], place, start)


def allowed_block(start, low, high, first_query):
    key = lax.broadcasted_iota(jnp.int32, (high - low, QB), 0) + low
    ok = key >= start
    if high > first_query:
        ok = ok & (key <= lax.broadcasted_iota(jnp.int32, (high - low, QB), 1) + first_query)
    return ok


def head_part(values, h):
    lane = lax.broadcasted_iota(jnp.int32, values.shape, 1)
    return jnp.where((lane < HEAD) if h == 0 else (lane >= HEAD), values, jnp.zeros_like(values))


def attend_kernel(scal, q_ref, k_ref, v_ref, o_ref, lse_ref, kb, vt):
    core = scal[CORE]
    rows = q_ref.shape[1]
    total = 2 * rows
    for half in range(2):
        rel = core ^ half
        kb[half * rows : (half + 1) * rows, :] = k_ref[rel]
        vt[:, half * rows : (half + 1) * rows] = v_ref[rel].T
    start = first_allowed(scal, total)
    for qb in range(total // QB):
        low = qb * QB
        rel = core ^ (low // rows)
        off = low % rows
        query = q_ref[rel, pl.ds(off, QB), :]
        begin = start[:, low : low + QB]
        parts = []
        for h in range(2):
            qh = head_part(query, h)
            cuts = [(0, low), (low, low + QB)] if low else [(0, QB)]
            scores = []
            peak = None
            for a, b in cuts:
                s = dot_nt(kb[a:b, :], qh)
                s = jnp.where(allowed_block(begin, a, b, low), s, -1e30)
                top = jnp.max(s, axis=0, keepdims=True)
                peak = top if peak is None else jnp.maximum(peak, top)
                scores.append(s)
            peak2 = peak * LOG2E
            summed, acc = None, None
            for (a, b), s in zip(cuts, scores):
                e = jnp.exp2(s * LOG2E - peak2)
                part = jnp.sum(e, axis=0, keepdims=True)
                prod = dot(vt[h * HEAD : (h + 1) * HEAD, a:b], e.astype(bf16))
                summed = part if summed is None else summed + part
                acc = prod if acc is None else acc + prod
            lse_ref[0, h : h + 1, low : low + QB] = peak2 + jnp.log2(summed)
            parts.append(acc / summed)
        o_ref[rel, pl.ds(off, QB), :] = jnp.concatenate(parts, axis=0).T.astype(bf16)


def attend(scal, q, k, v):
    _, rows, half = q.shape
    pairs = half // PAIR
    block = pl.BlockSpec((2, rows, PAIR), lambda p, sc: (0, 0, p))
    return pl.pallas_call(
        attend_kernel,
        grid_spec=pltpu.PrefetchScalarGridSpec(
            num_scalar_prefetch=1,
            grid=(pairs,),
            in_specs=[block] * 3,
            out_specs=[block, pl.BlockSpec((1, 8, 2 * rows), lambda p, sc: (p, 0, 0))],
            scratch_shapes=[pltpu.VMEM((2 * rows, PAIR), bf16), pltpu.VMEM((PAIR, 2 * rows), bf16)],
        ),
        out_shape=[sds((2, rows, half), bf16), sds((pairs, 8, 2 * rows), f32)],
        compiler_params=params(40, 1),
    )(scal, q, k, v)


def mlp_kernel(
    scal, att_own, att_oth, tok, cot, wo, bo, gain, shift, up, ub, down, db,
    out_ref, gm_ref, ga_keep, ga_send, dn_keep, dn_send, up_keep, up_send, ow_keep, ow_send, vec_ref,
    mid, xhat_ref, scale_ref, normed, acc, back, dtile,
):
    step, sub = pl.program_id(0), pl.program_id(1)
    steps = pl.num_programs(0)
    core = scal[CORE]
    width = tok.shape[1]
    half = width // 2
    chunk = width // 16
    fchunk = half // 2

    def att_weight(which):
        return wo[pl.ds(pl.multiple_of(which * half, half), half), :]

    @pl.when((step == 0) & (sub == 0))
    def _():
        branch = dot(att_own[...], att_weight(core)) + dot(att_oth[...], att_weight(1 - core)) + row_of(bo)
        middle = tok[...].astype(f32) + branch
        xhat, scale = normalise(middle)
        mid[...] = middle
        xhat_ref[...] = xhat
        scale_ref[...] = scale
        normed[...] = (xhat * row_of(gain) + row_of(shift)).astype(bf16)
        acc[...] = jnp.zeros_like(acc)
        back[...] = jnp.zeros_like(back)
        vec_ref[...] = jnp.zeros_like(vec_ref)

    @pl.when(sub == 0)
    def _():
        tile = (step + (steps // 2) * (1 - core)) & (steps - 1)
        v = dot(normed[...], up[...]) + ub[...].astype(f32)
        sq = v * v
        t = jnp.tanh(v * (GELU_C + (GELU_C * GELU_A) * sq))
        half_t = 0.5 * (1.0 + t)
        act = (v * half_t).astype(bf16)
        slope = half_t + (0.5 * v) * (1.0 - t * t) * (GELU_C + (3.0 * GELU_C * GELU_A) * sq)
        acc[...] += dot(act, down[...])
        dtile[...] = dot_tn(act, cot[...]).astype(bf16).reshape(2, fchunk, width)
        grad = (dot_nt(cot[...], down[...]) * slope).astype(bf16)
        back[...] += dot_nt(grad, up[...])
        vec_ref[pl.ds(V_UP + tile, 1), :] = jnp.sum(grad.astype(f32), axis=0, keepdims=True)
        dup = dot_tn(normed[...], grad).astype(bf16).reshape(16, chunk, half)

        @pl.when(step < steps // 2)
        def _():
            for d in range(16):
                up_send[scal[PLACE_OTH + d], 0] = dup[d]

        @pl.when(step >= steps // 2)
        def _():
            for d in range(16):
                up_keep[scal[PLACE + d], 0] = dup[d]

    for which in range(2):

        @pl.when((sub == which) & (core == 0))
        def _():
            dn_keep[0] = dtile[which, :, :half]
            dn_send[0] = dtile[which, :, half:]

        @pl.when((sub == which) & (core != 0))
        def _():
            dn_keep[0] = dtile[which, :, half:]
            dn_send[0] = dtile[which, :, :half]

    @pl.when((step == steps - 1) & (sub == 1))
    def _():
        out_ref[...] = (mid[...] + acc[...] + row_of(db)).astype(bf16)
        g = back[...]
        xhat = xhat_ref[...]
        grad_out = cot[...].astype(f32)
        weighted = g * row_of(gain)
        dv = scale_ref[...] * (
            weighted
            - jnp.mean(weighted, axis=-1, keepdims=True)
            - xhat * jnp.mean(weighted * xhat, axis=-1, keepdims=True)
        )
        grad_middle = grad_out + dv
        gm_ref[...] = grad_middle
        branch = grad_middle.astype(bf16)

        def put(row, vector):
            vec_ref[row : row + 1, :] = vector[:, :half]
            vec_ref[row + 1 : row + 2, :] = vector[:, half:]

        put(V_DOWN, jnp.sum(grad_out, axis=0, keepdims=True))
        put(V_OUT, jnp.sum(branch.astype(f32), axis=0, keepdims=True))
        put(V_GAIN2, jnp.sum(g * xhat, axis=0, keepdims=True))
        put(V_SHIFT2, jnp.sum(g, axis=0, keepdims=True))
        ga_keep[...] = dot_nt(branch, att_weight(core)).astype(bf16)
        ga_send[...] = dot_nt(branch, att_weight(1 - core)).astype(bf16)
        wide_own = dot_tn(att_own[...], branch).astype(bf16).reshape(8, chunk, width)
        wide_oth = dot_tn(att_oth[...], branch).astype(bf16).reshape(8, chunk, width)

        def spread(keep, send):
            for d in range(8):
                own_place = scal[PLACE + core * 8 + d]
                oth_place = scal[PLACE + (1 - core) * 8 + d]
                ow_keep[own_place] = wide_own[d, :, keep]
                ow_keep[oth_place] = wide_oth[d, :, keep]
                ow_send[scal[PLACE_OTH + core * 8 + d]] = wide_own[d, :, send]
                ow_send[scal[PLACE_OTH + (1 - core) * 8 + d]] = wide_oth[d, :, send]

        left, right = slice(0, half), slice(half, width)
        pl.when(core == 0)(lambda: spread(left, right))
        pl.when(core != 0)(lambda: spread(right, left))


def mlp(scal, att_own, att_oth, tok, cot, wo, bo, gain, shift, up, ub, down, db):
    rows, width = tok.shape
    half = width // 2
    hidden = up.shape[1]
    steps = hidden // half
    tile = lambda s, sc: (s + (steps // 2) * (1 - sc[CORE])) & (steps - 1)
    place = lambda s, j, sc: (sc[PLACE + 2 * tile(s, sc) + j], 0, 0)
    place_oth = lambda s, j, sc: (sc[PLACE_OTH + 2 * tile(s, sc) + j], 0, 0)
    return pl.pallas_call(
        mlp_kernel,
        grid_spec=pltpu.PrefetchScalarGridSpec(
            num_scalar_prefetch=1,
            grid=(steps, 2),
            in_specs=[
                whole((rows, half)),
                whole((rows, half)),
                whole((rows, width)),
                whole((rows, width)),
                whole((width, width)),
                whole((width,)),
                whole((width,)),
                whole((width,)),
                pl.BlockSpec((width, half), lambda s, j, sc: (0, tile(s, sc))),
                pl.BlockSpec((1, half), lambda s, j, sc: (0, tile(s, sc))),
                pl.BlockSpec((half, width), lambda s, j, sc: (tile(s, sc), 0)),
                whole((width,)),
            ],
            out_specs=[
                whole((rows, width)),
                whole((rows, width)),
                whole((rows, half)),
                whole((rows, half)),
                pl.BlockSpec((1, half // 2, half), place),
                pl.BlockSpec((1, half // 2, half), place_oth),
                pl.BlockSpec((16, 1, width // 16, half), lambda s, j, sc: (0, jnp.maximum(s - steps // 2, 0), 0, 0)),
                pl.BlockSpec((16, 1, width // 16, half), lambda s, j, sc: (0, jnp.minimum(s, steps // 2 - 1), 0, 0)),
                whole((16, width // 16, half)),
                whole((16, width // 16, half)),
                whole((16, half)),
            ],
            scratch_shapes=[
                pltpu.VMEM((rows, width), f32),
                pltpu.VMEM((rows, width), f32),
                pltpu.VMEM((rows, 1), f32),
                pltpu.VMEM((rows, width), bf16),
                pltpu.VMEM((rows, width), f32),
                pltpu.VMEM((rows, width), f32),
                pltpu.VMEM((2, half // 2, width), bf16),
            ],
        ),
        out_shape=[
            sds((rows, width), bf16),
            sds((rows, width), f32),
            sds((rows, half), bf16),
            sds((rows, half), bf16),
            sds((16, half // 2, half), bf16),
            sds((16, half // 2, half), bf16),
            sds((16, steps // 2, width // 16, half), bf16),
            sds((16, steps // 2, width // 16, half), bf16),
            sds((16, width // 16, half), bf16),
            sds((16, width // 16, half), bf16),
            sds((16, half), f32),
        ],
        compiler_params=params(52, 2),
    )(scal, att_own, att_oth, tok, cot, wo, bo, gain, shift, up, ub.reshape(1, -1), down, db)


def pair_back(scal, q_ref, k_ref, v_ref, o_ref, lse_ref, do1, do2, n_ref, wq_ref, wk_ref, wv_ref, dv_ref, scratch):
    kb, vb, kt, db, dk_acc, dv_acc, x = scratch
    core = scal[CORE]
    rows = q_ref.shape[1]
    total = 2 * rows
    width = n_ref.shape[2]
    for hf in range(2):
        rel = core ^ hf
        cut = slice(hf * rows, (hf + 1) * rows)
        kb[cut, :] = k_ref[rel]
        vb[cut, :] = v_ref[rel]
        kt[:, cut] = k_ref[rel].T
    db[0] = do1[...]
    db[1] = do2[...]
    dk_acc[...] = jnp.zeros_like(dk_acc)
    dv_acc[...] = jnp.zeros_like(dv_acc)
    start = first_allowed(scal, total)
    for qb in range(total // QB):
        low = qb * QB
        rel = core ^ (low // rows)
        off = low % rows
        query = q_ref[rel, pl.ds(off, QB), :]
        grad = db[rel, pl.ds(off, QB), :]
        prod = (grad.astype(f32) * o_ref[rel, pl.ds(off, QB), :].astype(f32)).T
        begin = start[:, low : low + QB]
        parts = []
        for h in range(2):
            qh = head_part(query, h)
            gh = head_part(grad, h)
            delta = jnp.sum(prod[h * HEAD : (h + 1) * HEAD], axis=0, keepdims=True)
            total_log = lse_ref[0, h : h + 1, low : low + QB]
            acc = None
            for a, b in [(0, low), (low, low + QB)] if low else [(0, QB)]:
                s = dot_nt(kb[a:b, :], qh)
                p = jnp.where(allowed_block(begin, a, b, low), jnp.exp2(s * LOG2E - total_log), 0.0)
                dp = dot_nt(vb[a:b, :], gh)
                ds = (p * (dp - delta)).astype(bf16)
                dv_acc[a:b, :] += dot(p.astype(bf16), gh)
                dk_acc[a:b, :] += dot(ds, qh)
                part = dot(kt[h * HEAD : (h + 1) * HEAD, a:b], ds)
                acc = part if acc is None else acc + part
            parts.append(acc)
        x[rel, pl.ds(off, QB), 0:PAIR] = (jnp.concatenate(parts, axis=0).T * (HEAD**-0.5)).astype(bf16)
    for hf in range(2):
        rel = core ^ hf
        cut = slice(hf * rows, (hf + 1) * rows)
        x[rel, :, PAIR : 2 * PAIR] = dk_acc[cut, :].astype(bf16)
        dv = dv_acc[cut, :].astype(bf16)
        dv_ref[rel] = dv
        x[rel, :, 2 * PAIR :] = jnp.where(core == 0, dv, jnp.zeros_like(dv))
    grads = x[...].reshape(total, 3 * PAIR)
    dw = dot_tn(n_ref[...].reshape(total, width), grads).astype(bf16).reshape(16, width // 16, 3 * PAIR)
    back = (
        dot_nt(grads[:, :PAIR], wq_ref[...])
        + dot_nt(grads[:, PAIR : 2 * PAIR], wk_ref[...])
        + dot_nt(grads[:, 2 * PAIR :], wv_ref[...])
    )
    return dw, back, jnp.sum(grads.astype(f32), axis=0, keepdims=True)


def early_pairs_kernel(scal, *refs):
    inputs, (ow_keep, ow_recv), (t_ref, gn_ref, dv_ref, sums_ref), scratch = refs[:11], refs[11:13], refs[13:17], refs[17:]
    step = pl.program_id(0)
    dw, back, sums = pair_back(scal, *inputs, dv_ref, scratch)
    for d in range(16):
        t_ref[scal[PLACE + d], step] = dw[d]

    @pl.when(step == 0)
    def _():
        gn_ref[...] = back
        sums_ref[0:1, :] = sums
        t_ref[:, 2] = (ow_keep[...].astype(f32) + ow_recv[...].astype(f32)).astype(bf16)

    @pl.when(step != 0)
    def _():
        gn_ref[...] += back
        sums_ref[1:2, :] = sums


def last_pair_kernel(scal, *refs):
    inputs, (gn_in, sums_in, vec_in, own, oth), (t_ref, gn_ref, gs_ref, dv_ref), scratch = refs[:11], refs[11:16], refs[16:20], refs[20:]
    core = scal[CORE]
    dw, back, sums = pair_back(scal, *inputs, dv_ref, scratch)
    for d in range(16):
        t_ref[scal[PLACE + d]] = dw[d]
    rows = own.shape[0]
    half = own.shape[1] // 2
    g = back + gn_in[...]
    gn_ref[...] = g[:rows]
    gs_ref[...] = g[rows:].astype(bf16)
    gains, shifts = 0.0, 0.0
    for rel, tok in ((0, own), (1, oth)):
        xhat, _ = normalise(tok[...].astype(f32))
        part = g[rel * rows : (rel + 1) * rows]
        gains += jnp.sum(part * xhat, axis=0, keepdims=True)
        shifts += jnp.sum(part, axis=0, keepdims=True)
    every = [sums_in[0:1, :], sums_in[1:2, :], sums]
    query_bias = jnp.concatenate([s[:, :PAIR] for s in every], axis=1)
    value_bias = jnp.concatenate([s[:, 2 * PAIR :] for s in every], axis=1)
    none = jnp.zeros_like(query_bias)
    vec = [vec_in[...], gains[:, :half], gains[:, half:], shifts[:, :half], shifts[:, half:]]
    vec += [jnp.where(core == 0, query_bias, none), jnp.where(core == 0, none, query_bias), value_bias, none]
    t_ref[16] = split_high_low(jnp.concatenate(vec, axis=0))


def split_high_low(vec):
    high = vec.astype(bf16)
    return jnp.concatenate([high, (vec - high.astype(f32)).astype(bf16)], axis=0)


def join_high_low(block):
    return block[:V_ROWS].astype(f32) + block[V_ROWS:].astype(f32)


def back_specs(pairs_before, rows, width):
    half = width // 2
    pairs = half // PAIR
    pair = lambda p: p + pairs_before
    head = pl.BlockSpec((2, rows, PAIR), lambda p, sc: (0, 0, pair(p)))
    rel = pl.BlockSpec((rows, PAIR), lambda p, sc: (0, pair(p)))
    weight = pl.BlockSpec((width, PAIR), lambda p, sc: (0, sc[CORE] * pairs + pair(p)))
    in_specs = [head] * 4 + [
        pl.BlockSpec((1, 8, 2 * rows), lambda p, sc: (pair(p), 0, 0)),
        rel,
        rel,
        whole((2, rows, width)),
        weight,
        weight,
        pl.BlockSpec((width, PAIR), lambda p, sc: (0, pair(p))),
    ]
    scratch = [
        pltpu.VMEM((2 * rows, PAIR), bf16),
        pltpu.VMEM((2 * rows, PAIR), bf16),
        pltpu.VMEM((PAIR, 2 * rows), bf16),
        pltpu.VMEM((2, rows, PAIR), bf16),
        pltpu.VMEM((2 * rows, PAIR), f32),
        pltpu.VMEM((2 * rows, PAIR), f32),
        pltpu.VMEM((2, rows, 3 * PAIR), bf16),
    ]
    return in_specs, scratch


def early_pairs(scal, head_args, ow_keep, ow_recv):
    rows, width = head_args[7].shape[1:]
    half = width // 2
    in_specs, scratch = back_specs(0, rows, width)
    share = (16, width // 16, half)
    return pl.pallas_call(
        early_pairs_kernel,
        grid_spec=pltpu.PrefetchScalarGridSpec(
            num_scalar_prefetch=1,
            grid=(2,),
            in_specs=in_specs + [whole(share)] * 2,
            out_specs=[
                whole((16, 3, width // 16, half)),
                whole((2 * rows, width)),
                pl.BlockSpec((2, rows, PAIR), lambda p, sc: (0, 0, p)),
                whole((8, half)),
            ],
            scratch_shapes=scratch,
        ),
        out_shape=[
            sds((16, 3, width // 16, half), bf16),
            sds((2 * rows, width), f32),
            sds((2, rows, 2 * PAIR), bf16),
            sds((8, half), f32),
        ],
        compiler_params=params(48, 1),
    )(scal, *head_args, ow_keep, ow_recv)


def last_pair(scal, head_args, gn, sums, vec, own, oth):
    rows, width = own.shape
    half = width // 2
    in_specs, scratch = back_specs(2, rows, width)
    return pl.pallas_call(
        last_pair_kernel,
        grid_spec=pltpu.PrefetchScalarGridSpec(
            num_scalar_prefetch=1,
            grid=(1,),
            in_specs=in_specs
            + [whole((2 * rows, width)), whole((8, half)), whole((16, half)), whole((rows, width)), whole((rows, width))],
            out_specs=[
                whole((17, width // 16, half)),
                whole((rows, width)),
                whole((rows, width)),
                whole((2, rows, PAIR)),
            ],
            scratch_shapes=scratch,
        ),
        out_shape=[
            sds((17, width // 16, half), bf16),
            sds((rows, width), f32),
            sds((rows, width), bf16),
            sds((2, rows, PAIR), bf16),
        ],
        compiler_params=params(48, 1),
    )(scal, *head_args, gn, sums, vec, own, oth)


def first_norm_back_kernel(tok, gain, gn_own, gn_oth, grad_middle, out_ref):
    xhat, scale = normalise(tok[...].astype(f32))
    weighted = (gn_own[...] + gn_oth[...].astype(f32)) * row_of(gain)
    dv = scale * (
        weighted
        - jnp.mean(weighted, axis=-1, keepdims=True)
        - xhat * jnp.mean(weighted * xhat, axis=-1, keepdims=True)
    )
    out_ref[...] = (grad_middle[...] + dv).astype(bf16)


def first_norm_back(tok, gain, gn_own, gn_oth, grad_middle):
    rows, width = tok.shape
    tile = rows // 2
    block = pl.BlockSpec((tile, width), lambda s: (s, 0))
    return pl.pallas_call(
        first_norm_back_kernel,
        grid=(2,),
        in_specs=[block, whole((width,)), block, block, block],
        out_specs=block,
        out_shape=sds((rows, width), bf16),
        compiler_params=params(40, 1),
    )(tok, gain, gn_own, gn_oth, grad_middle)


def flip(values, bits, dp_count):
    pairs = [((d * 2 + c), ((d ^ bits[c]) * 2 + c)) for d in range(dp_count) for c in range(2)]
    return lax.ppermute(values, ("dp", "seq"), pairs)


def swap(values):
    return lax.ppermute(values, "seq", [(0, 1), (1, 0)])


STAGES = ((1, 2), (2, 1), (4, 4), (8, 8))


def halve(buffer):
    for bits in STAGES:
        half = buffer.shape[0] // 2
        buffer = buffer[:half] + flip(buffer[half:], bits, 16)
    return buffer


def add_with_vec_kernel(mine, theirs, out):
    count = out.shape[0] - 1
    out[:count] = mine[:count] + theirs[:count]
    out[count] = split_high_low(join_high_low(mine[2 * count]) + join_high_low(theirs[count]))


def halve_with_vec(buffer):
    for bits in STAGES:
        half = (buffer.shape[0] - 1) // 2
        theirs = flip(buffer[half:], bits, 16)
        buffer = pl.pallas_call(
            add_with_vec_kernel,
            out_shape=sds((half + 1,) + buffer.shape[1:], bf16),
            compiler_params=pltpu.CompilerParams(vmem_limit_bytes=32 << 20),
        )(buffer, theirs)
    return buffer


def finish_kernel(scal, *refs):
    (down, up, early, late, down2, up2, early2, late2), outs = refs[:8], refs[8:]
    gq, gk, gv, go, gu, gd = outs[:6]
    vec_out = outs[6:]
    half = down.shape[1]
    core = scal[CORE]

    def place(side, down, up, early, late):
        at = side * half
        gd[:, at : at + half] = down[...].astype(f32)
        for g in range(up.shape[0]):
            gu[:, (side * up.shape[0] + g) * half : (side * up.shape[0] + g + 1) * half] = up[g].astype(f32)
        go[:, at : at + half] = early[2].astype(f32)
        for p, piece in enumerate((early[0], early[1], late[0])):
            cols = slice(at + p * PAIR, at + (p + 1) * PAIR)
            gq[:, cols] = piece[:, :PAIR].astype(f32)
            gk[:, cols] = piece[:, PAIR : 2 * PAIR].astype(f32)
            if side == 0:
                gv[:, p * PAIR : (p + 1) * PAIR] = piece[:, 2 * PAIR :].astype(f32)

    @pl.when(core == 0)
    def _():
        place(0, down, up, early, late)
        place(1, down2, up2, early2, late2)

    @pl.when(core != 0)
    def _():
        place(1, down, up, early, late)
        place(0, down2, up2, early2, late2)

    put_vectors(join_high_low(late[1]) + join_high_low(late2[1]), vec_out)


def put_vectors(vec, refs):
    for ref, row in zip(refs, (V_GAIN1, V_SHIFT1, V_QUERY, V_VALUE, V_OUT, V_GAIN2, V_SHIFT2, V_UP, V_DOWN)):
        for k in range(ref.shape[0] // vec.shape[1]):
            ref[k * vec.shape[1] : (k + 1) * vec.shape[1]] = vec[row + k]


def finish(scal, own, oth, width, hidden, dp_count):
    half = width // 2
    rows = width // dp_count
    out_shape = [
        sds((rows, width), f32),
        sds((rows, width), f32),
        sds((rows, half), f32),
        sds((rows, width), f32),
        sds((rows, hidden), f32),
        sds((hidden // dp_count, width), f32),
    ] + [sds((n,), f32) for n in (width, width, width, half, width, width, width, hidden, width)]
    return pl.pallas_call(
        finish_kernel,
        grid_spec=pltpu.PrefetchScalarGridSpec(
            num_scalar_prefetch=1,
            grid=(1,),
            in_specs=[whole(x.shape) for x in own + oth],
            out_specs=[whole(s.shape) for s in out_shape],
        ),
        out_shape=out_shape,
        compiler_params=params(40, 1),
    )(scal, *own, *oth)


def finish_any(core, down, up, early, late):
    half = down.shape[2]
    vec = lax.psum(join_high_low(late[16]), ("dp", "seq"))

    def columns(pieces):
        mine = jnp.concatenate([x.reshape(-1, x.shape[-1]).astype(f32) for x in pieces], axis=1)
        share = lax.psum_scatter(mine, "dp", scatter_dimension=0, tiled=True)
        other = swap(share)
        return jnp.where(core == 0, jnp.concatenate([share, other], 1), jnp.concatenate([other, share], 1))

    thirds = [early[:, 0], early[:, 1], late[:16]]
    gq, gk, gv = (columns([x[..., i * PAIR : (i + 1) * PAIR] for x in thirds]) for i in range(3))
    go = columns([early[:, 2]])
    gu = columns([up[:, g] for g in range(up.shape[1])])
    gd = columns([down])
    flat = lambda row, n: vec[row : row + n].reshape(-1)
    vectors = [flat(V_GAIN1, 2), flat(V_SHIFT1, 2), flat(V_QUERY, 2), flat(V_VALUE, 1), flat(V_OUT, 2)]
    vectors += [flat(V_GAIN2, 2), flat(V_SHIFT2, 2), flat(V_UP, 8), flat(V_DOWN, 2)]
    return [gq, gk, gv[:, :half], go, gu, gd] + vectors


def per_device(
    dp_count,
    tokens,
    skip_values,
    doc_lengths,
    gain_first,
    shift_first,
    query_weight,
    query_bias,
    key_weight,
    value_weight,
    value_bias,
    out_weight,
    out_bias,
    gain_second,
    shift_second,
    up_weight,
    up_bias,
    down_weight,
    down_bias,
    cotangent,
):
    rows, width = tokens.shape
    hidden = up_weight.shape[1]
    core = lax.axis_index("seq")
    chunks = jnp.arange(16, dtype=jnp.int32)
    if dp_count == 16:
        off = chunks ^ lax.axis_index("dp")
        x_bit, y_bit, z_bits = off & 1, (off >> 1) & 1, ((off >> 2) & 1) * 2 + ((off >> 3) & 1)
        x_first, y_first = x_bit * 8 + y_bit * 4 + z_bits, y_bit * 8 + x_bit * 4 + z_bits
        place, place_oth = jnp.where(core == 0, x_first, y_first), jnp.where(core == 0, y_first, x_first)
    else:
        place = place_oth = chunks
    bounds = jnp.cumsum(doc_lengths[0])[:5]
    scal = jnp.concatenate([core[None], place, bounds, place_oth]).astype(jnp.int32)

    tokens_oth = swap(tokens)
    skip_oth = swap(skip_values)
    q, k, v, normed = project(
        scal, tokens, tokens_oth, skip_values, skip_oth, gain_first, shift_first,
        query_weight, query_bias, key_weight, value_weight, value_bias,
    )
    attended, log_total = attend(scal, q, k, v)
    att_oth = swap(attended[1])
    (output, grad_middle, ga_keep, ga_send, dn_keep, dn_send, up_keep, up_send, ow_keep, ow_send, vec) = mlp(
        scal, attended[0], att_oth, tokens, cotangent, out_weight, out_bias, gain_second, shift_second,
        up_weight, up_bias, down_weight, down_bias,
    )
    ga_oth = swap(ga_send)
    ow_recv = swap(ow_send)
    down_sum = dn_keep + swap(dn_send)
    up_sum = up_keep + swap(up_send)
    head_args = (q, k, v, attended, log_total, ga_keep, ga_oth, normed, query_weight, key_weight, value_weight)
    early, gn, dv_early, sums = early_pairs(scal, head_args, ow_keep, ow_recv)
    late, gn_own, gn_send, dv_late = last_pair(scal, head_args, gn, sums, vec, tokens, tokens_oth)
    grad_tokens = first_norm_back(tokens, gain_first, gn_own, swap(gn_send), grad_middle)
    dv = jnp.concatenate([dv_early, dv_late], axis=2)
    dv_oth = lax.ppermute(dv[1], "seq", [(1, 0)])
    grad_skip = jnp.where(core == 0, dv_oth, dv[0])
    if dp_count == 16:
        own = [halve(down_sum)[0], halve(up_sum)[0], halve(early)[0], halve_with_vec(late)]
        oth = [swap(x) for x in own]
        rest = finish(scal, own, oth, width, hidden, dp_count)
    else:
        rest = finish_any(core, down_sum, up_sum, early, late)
    gq, gk, gv, go, gu, gd, gain1, shift1, gqb, gvb, gob, gain2, shift2, gub, gdb = rest
    return (
        output, grad_tokens, grad_skip, gain1, shift1, gq, gqb, gk, gv, gvb, go, gob, gain2, shift2, gu, gub, gd, gdb,
    )


def solution(mesh):
    rows, full, shares = P(("dp", "seq"), None), P(), P("dp", None)
    return jax.shard_map(
        functools.partial(per_device, mesh.shape["dp"]),
        mesh=mesh,
        in_specs=(rows, rows, shares) + (full,) * 15 + (rows,),
        out_specs=(
            rows, rows, rows, full, full, shares, full, shares, shares, full, shares, full, full, full, shares, full,
            shares, full,
        ),
        check_vma=False,
    )
```

time: 1050 us -> 209 us (0.20)
  waiting for transfers between devices: 658 us -> 66.6 us
  matrix products: 169 us -> 0 us
  Pallas kernels: 0 us -> 96.5 us
  blocking collectives: 68.3 us -> 0 us
  local copies, waits for them, and re-layouts: 55.9 us -> 12.9 us
  other arithmetic: 40.6 us -> 5.39 us
  loops' own time: 19.7 us -> 0 us
  between operations: 15.2 us -> 1.29 us
    reduce_scatter x6 -> x0, waiting for transfers between devices: 638 us -> none  [the longest x1 175 us: per_device(): lax.psum_scatter(matrices[4], 'dp', scatter_dimension=0, tiled=True)]
    dot_general x60 -> x0, matrix products: 169 us -> none  [the longest x12 46.2 us: head_scores(): jnp.einsum('qd,kd->qk', query_part, key_part, preferred_element_type=f32)]
    pallas_call x0 -> x11, Pallas kernels: none -> 96.5 us  [the longest x1 43.9 us: mlp(): pl.pallas_call(mlp_kernel, grid_spec=pltpu.PrefetchScalarGridSpec(num_sca...]
    ppermute x0 -> x29, waiting for transfers between devices: none -> 66.6 us  [the longest x16 55.4 us: flip(): return lax.ppermute(values, ('dp', 'seq'), pairs)]
    psum x2 -> x0, blocking collectives: 46.9 us -> none  [the longest x1 43.5 us: per_device(): lax.psum((grad_gain_first, grad_shift_first, grad_query_bias, grad_value_...]
    ppermute x0 -> x29, starting transfers between devices: none -> 25.4 us  [the longest x16 20.5 us: flip(): return lax.ppermute(values, ('dp', 'seq'), pairs)]
    convert_element_type x27 -> x0, other arithmetic: 24.3 us -> none  [the longest x6 6.81 us: differentiate(): grad_scores = (attention * (grad_probs - row_term)).astype(bf16)]
    all_to_all x4 -> x0, blocking collectives: 21.4 us -> none  [the longest x1 6.35 us: per_device(): lax.all_to_all(side_by_side(grad_value_heads), 'seq', split_axis=0, conca...]
  transfers between devices with their start and end apart: 11 -> 29, of which waited for: 8 -> 13; matrix products, arithmetic and copies ran while one was open for 16% -> 4% of each run, Pallas kernels for 0% -> 16%
where the time goes in v1:
time: 209 us; the launch traced here: 208 us
  Pallas kernels  96.5 us (46%)
  waiting for transfers between devices  66.6 us (32%)
  starting transfers between devices  25.4 us (12%)
  local copies, waits for them, and re-layouts  12.9 us (6%)
  other arithmetic  5.39 us (3%)
    ppermute x16, waiting for transfers between devices, flip(): return lax.ppermute(values, ('dp', 'seq'), pairs)  55.4 us
    pallas_call x1, Pallas kernels, mlp(): pl.pallas_call(mlp_kernel, grid_spec=pltpu.PrefetchScalarGridSpec(num_sca...  43.9 us
    ppermute x16, starting transfers between devices, flip(): return lax.ppermute(values, ('dp', 'seq'), pairs)  20.5 us
    pallas_call x1, Pallas kernels, early_pairs(): pl.pallas_call(early_pairs_kernel, grid_spec=pltpu.PrefetchScalarGridSpec...  19.6 us
    pallas_call x1, Pallas kernels, last_pair(): pl.pallas_call(last_pair_kernel, grid_spec=pltpu.PrefetchScalarGridSpec(n...  12.3 us
    ppermute x12, waiting for transfers between devices, swap(): return lax.ppermute(values, 'seq', [(0, 1), (1, 0)])  11.2 us
    pallas_call x1, Pallas kernels, attend(): pl.pallas_call(attend_kernel, grid_spec=pltpu.PrefetchScalarGridSpec(num_...  11.1 us
    unnamed x51, local copies, waits for them, and re-layouts  10.2 us
  transfers between devices with their start and end apart: 29, of which 13 were waited for; matrix products, arithmetic and copies ran while one was open for 4% of the time, Pallas kernels for 16%

profile of v1, /device:TPU:0, one launch (start us, length us, event | category | flops | bytes accessed | tf_op | source)
XLA Modules:
  0.0 208.2 jit_solution(10755392152307623891)
XLA Ops:
  11.6 5.6 %shard_map.322 = (bf16[2,512,384]{2,1,0:T(8,128)(2,1)S(1)}, bf16[2,512,384]{2,1,0:T(8,128)(2,1)S(1)}, bf16[2,512,384]{2,1,0:T(8,128)(2,1)S(1)}, bf16[2,512,768]{2,1,0:T(8,128)(2,1)S(1)}) custom-call(s32[38]{0:T(128)S(1)} %pad_add_fusion.scal, bf16[512,768]{1,0:T(8,128)(2,1)S(1)} %copy-done, bf16[512,768]{1,0:T(8,128)(2,1)S(1)} %collective-permute-done.oth.refs_15_, ...), custom_call_target="tpu_custom_call" | custom-call | tf_op jit(solution)/shard_map/pallas_call | solution.py:89
  17.3 11.1 %shard_map.323 = (bf16[2,512,384]{2,1,0:T(8,128)(2,1)S(1)}, f32[3,8,1024]{2,1,0:T(8,128)S(1)}) custom-call(s32[38]{0:T(128)S(1)} %pad_add_fusion.scal, bf16[2,512,384]{2,1,0:T(8,128)(2,1)S(1)} %get-tuple-element.58.q_ref.refs_0_, bf16[2,512,384]{2,1,0:T(8,128)(2,1)S(1)} %get-tuple-element.59.k_ref.refs_1_, ...), custom_call_target="tpu_custom_call" | custom-call | tf_op jit(solution)/shard_map/pallas_call | solution.py:179
  28.7 1.7 collective-permute-done.2.att_oth
  30.4 43.9 %shard_map.324 = (bf16[512,768]{1,0:T(8,128)(2,1)}, f32[512,768]{1,0:T(8,128)}, bf16[512,384]{1,0:T(8,128)(2,1)S(1)}, bf16[512,384]{1,0:T(8,128)(2,1)S(1)}, bf16...) custom-call(s32[38]{0:T(128)S(1)} %pad_add_fusion.scal, ...), custom_call_target="tpu_custom_call" | custom-call | tf_op jit(solution)/shard_map/pallas_call | solution.py:311
  75.4 4.6 %collective-permute-done.3.refs_6_ = bf16[512,384]{1,0:T(8,128)(2,1)S(1)} collective-permute-done((bf16[512,384]{1,0:T(8,128)(2,1)S(1)}, bf16[512,384]{1,0:T(8,128)(2,1)S(1)}, u32[]{:S(2)}, u32[]{:S(2)}) %collective-permute-start.3) | collective-permute-done | bytes 393248 | tf_op jit(solution)/shard_map/ppermute | solution.py:601
  80.0 3.9 %collective-permute-done.4.refs_12_ = bf16[16,48,384]{2,1,0:T(8,128)(2,1)S(1)} collective-permute-done((bf16[16,48,384]{2,1,0:T(8,128)(2,1)}, bf16[16,48,384]{2,1,0:T(8,128)(2,1)S(1)}, u32[]{:S(2)}, u32[]{:S(2)}) %collective-permute-start.4) | collective-permute-done | bytes 589856 | tf_op jit(solution)/shard_map/ppermute | solution.py:601
  85.0 19.6 %shard_map.325 = (bf16[16,3,48,384]{3,2,1,0:T(8,128)(2,1)}, f32[1024,768]{1,0:T(8,128)}, bf16[2,512,256]{2,1,0:T(8,128)(2,1)S(1)}, f32[8,384]{1,0:T(8,128)S(1)}) custom-call(s32[38]{0:T(128)S(1)} %pad_add_fusion.scal, bf16[2,512,384]{2,1,0:T(8,128)(2,1)S(1)} %get-tuple-element.58.q_ref.refs_0_, bf16[2,512,384]{2,1,0:T(8,128)(2,1)S(1)} %get-tuple-element.59.k_ref.refs_1_, ...), custom_call_target="tpu_custom_call" | custom-call | tf_op jit(solution)/shard_map/pallas_call | solution.py:517
  105.8 2.9 %collective-permute-start.17 = (bf16[8,3,48,384]{3,2,1,0:T(8,128)(2,1)S(1)}, bf16[8,3,48,384]{3,2,1,0:T(8,128)(2,1)}, u32[]{:S(2)}, u32[]{:S(2)}) collective-permute-start(bf16[8,3,48,384]{3,2,1,0:T(8,128)(2,1)S(1)} %slice.125), channel_id=1, source_target_pairs={{0,2},{1,5},{2,0},{3,7},{4,6},{5,1},{6,4},{7,3},{8,10},{9,13},{10,... | collective-permute-start | bytes 2654216 | tf_op jit(solution)/shard_map/ppermute | solution.py:597
  109.7 12.3 %shard_map.326 = (bf16[17,48,384]{2,1,0:T(8,128)(2,1)S(1)}, f32[512,768]{1,0:T(8,128)}, bf16[512,768]{1,0:T(8,128)(2,1)S(1)}, bf16[2,512,128]{2,1,0:T(8,128)(2,1)S(1)}) custom-call(s32[38]{0:T(128)S(1)} %pad_add_fusion.scal, bf16[2,512,384]{2,1,0:T(8,128)(2,1)S(1)} %get-tuple-element.58.q_ref.refs_0_, ...), custom_call_target="tpu_custom_call" | custom-call | tf_op jit(solution)/shard_map/pallas_call | solution.py:545
  122.1 2.1 collective-permute-start.21
  129.4 11.3 %collective-permute-done.21.theirs = bf16[9,48,384]{2,1,0:T(8,128)(2,1)S(1)} collective-permute-done((bf16[9,48,384]{2,1,0:T(8,128)(2,1)S(1)}, bf16[9,48,384]{2,1,0:T(8,128)(2,1)S(1)}, u32[]{:S(2)}, u32[]{:S(2)}) %collective-permute-start.21) | collective-permute-done | bytes 331808 | tf_op jit(solution)/shard_map/ppermute | solution.py:597
  140.8 2.1 %collective-permute-start.22 = (bf16[5,48,384]{2,1,0:T(8,128)(2,1)S(1)}, bf16[5,48,384]{2,1,0:T(8,128)(2,1)S(1)}, u32[]{:S(2)}, u32[]{:S(2)}) collective-permute-start(bf16[5,48,384]{2,1,0:T(8,128)(2,1)S(1)} %slice.160), channel_id=1, source_target_pairs={{0,4},{1,3},{2,6},{3,1},{4,0},{5,7},{6,2},{7,5},{8,12},{9,11},{10,... | collective-permute-start | bytes 552968 | tf_op jit(solution)/shard_map/ppermute | solution.py:597
  142.9 5.5 %collective-permute-done.22.theirs = bf16[5,48,384]{2,1,0:T(8,128)(2,1)S(1)} collective-permute-done((bf16[5,48,384]{2,1,0:T(8,128)(2,1)S(1)}, bf16[5,48,384]{2,1,0:T(8,128)(2,1)S(1)}, u32[]{:S(2)}, u32[]{:S(2)}) %collective-permute-start.22) | collective-permute-done | bytes 184352 | tf_op jit(solution)/shard_map/ppermute | solution.py:597
  148.5 2.1 %collective-permute-start.23 = (bf16[3,48,384]{2,1,0:T(8,128)(2,1)S(1)}, bf16[3,48,384]{2,1,0:T(8,128)(2,1)S(1)}, u32[]{:S(2)}, u32[]{:S(2)}) collective-permute-start(bf16[3,48,384]{2,1,0:T(8,128)(2,1)S(1)} %slice.161), channel_id=1, source_target_pairs={{0,8},{1,9},{2,10},{3,11},{4,12},{5,13},{6,14},{7,15},{8,0},{9,1},... | collective-permute-start | bytes 331784 | tf_op jit(solution)/shard_map/ppermute | solution.py:597
  150.7 2.7 %collective-permute-done.23.theirs = bf16[3,48,384]{2,1,0:T(8,128)(2,1)S(1)} collective-permute-done((bf16[3,48,384]{2,1,0:T(8,128)(2,1)S(1)}, bf16[3,48,384]{2,1,0:T(8,128)(2,1)S(1)}, u32[]{:S(2)}, u32[]{:S(2)}) %collective-permute-start.23) | collective-permute-done | bytes 110624 | tf_op jit(solution)/shard_map/ppermute | solution.py:597
  153.5 3.2 %collective-permute-start.24 = (bf16[2,48,384]{2,1,0:T(8,128)(2,1)S(1)}, bf16[2,48,384]{2,1,0:T(8,128)(2,1)S(1)}, u32[]{:S(2)}, u32[]{:S(2)}) collective-permute-start(bf16[2,48,384]{2,1,0:T(8,128)(2,1)S(1)} %slice.162), channel_id=1, source_target_pairs={{0,16},{1,17},{2,18},{3,19},{4,20},{5,21},{6,22},{7,23},{8,24},{9,... | collective-permute-start | bytes 221192 | tf_op jit(solution)/shard_map/ppermute | solution.py:597
  163.7 4.8 %collective-permute-done.9 = bf16[4,192,384]{2,1,0:T(8,128)(2,1)S(1)} collective-permute-done((bf16[4,192,384]{2,1,0:T(8,128)(2,1)S(1)}, bf16[4,192,384]{2,1,0:T(8,128)(2,1)S(1)}, u32[]{:S(2)}, u32[]{:S(2)}) %collective-permute-start.9) | collective-permute-done | bytes 589856 | tf_op jit(solution)/shard_map/ppermute | solution.py:597
  169.0 5.8 %collective-permute-done.14 = bf16[4,4,48,384]{3,2,1,0:T(8,128)(2,1)S(1)} collective-permute-done((bf16[4,4,48,384]{3,2,1,0:T(8,128)(2,1)S(1)}, bf16[4,4,48,384]{3,2,1,0:T(8,128)(2,1)S(1)}, u32[]{:S(2)}, u32[]{:S(2)}) %collective-permute-start.14) | collective-permute-done | bytes 589856 | tf_op jit(solution)/shard_map/ppermute | solution.py:597
  177.1 6.8 %collective-permute-done.10 = bf16[2,192,384]{2,1,0:T(8,128)(2,1)S(1)} collective-permute-done((bf16[2,192,384]{2,1,0:T(8,128)(2,1)S(1)}, bf16[2,192,384]{2,1,0:T(8,128)(2,1)S(1)}, u32[]{:S(2)}, u32[]{:S(2)}) %collective-permute-start.10) | collective-permute-done | bytes 294944 | tf_op jit(solution)/shard_map/ppermute | solution.py:597
  184.0 3.0 %collective-permute-done.15 = bf16[2,4,48,384]{3,2,1,0:T(8,128)(2,1)S(1)} collective-permute-done((bf16[2,4,48,384]{3,2,1,0:T(8,128)(2,1)S(1)}, bf16[2,4,48,384]{3,2,1,0:T(8,128)(2,1)S(1)}, u32[]{:S(2)}, u32[]{:S(2)}) %collective-permute-start.15) | collective-permute-done | bytes 294944 | tf_op jit(solution)/shard_map/ppermute | solution.py:597
  187.4 9.3 %collective-permute-done.11 = bf16[1,192,384]{2,1,0:T(8,128)(2,1)S(1)} collective-permute-done((bf16[1,192,384]{2,1,0:T(8,128)(2,1)S(1)}, bf16[1,192,384]{2,1,0:T(8,128)(2,1)S(1)}, u32[]{:S(2)}, u32[]{:S(2)}) %collective-permute-start.11) | collective-permute-done | bytes 147488 | tf_op jit(solution)/shard_map/ppermute | solution.py:597
  196.7 6.0 %collective-permute-done.16 = bf16[1,4,48,384]{3,2,1,0:T(8,128)(2,1)S(1)} collective-permute-done((bf16[1,4,48,384]{3,2,1,0:T(8,128)(2,1)S(1)}, bf16[1,4,48,384]{3,2,1,0:T(8,128)(2,1)S(1)}, u32[]{:S(2)}, u32[]{:S(2)}) %collective-permute-start.16) | collective-permute-done | bytes 147488 | tf_op jit(solution)/shard_map/ppermute | solution.py:597
  204.2 1.9 shard_map.327
  206.1 1.9 shard_map.332
  (136 shorter events, 32.6 us)
Async XLA Ops:
  74.3 34.4 %collective-permute-start.7 = (bf16[16,192,384]{2,1,0:T(8,128)(2,1)}, bf16[16,192,384]{2,1,0:T(8,128)(2,1)S(1)}, u32[]{:S(2)}, u32[]{:S(2)}) collective-permute-start(bf16[16,192,384]{2,1,0:T(8,128)(2,1)} %get-tuple-element.78), channel_id=1, source_target_pairs={{0,1},{1,0},{2,3},{3,2},{4,5},{5,4},{6,7},{7,6},{8,9},{9,8},{10,11... | collective-permute-start | bytes 7077896 | tf_op jit(solution)/shard_map/ppermute | solution.py:601
  74.5 49.7 %collective-permute-start.12 = (bf16[16,4,48,384]{3,2,1,0:T(8,128)(2,1)}, bf16[16,4,48,384]{3,2,1,0:T(8,128)(2,1)S(1)}, u32[]{:S(2)}, u32[]{:S(2)}) collective-permute-start(bf16[16,4,48,384]{3,2,1,0:T(8,128)(2,1)} %get-tuple-element.80), channel_id=1, source_target_pairs={{0,1},{1,0},{2,3},{3,2},{4,5},{5,4},{6,7},{7,6},{8,9},{9,8},{10,11... | collective-permute-start | bytes 7077896 | tf_op jit(solution)/shard_map/ppermute | solution.py:601
  74.9 9.0 %collective-permute-start.4 = (bf16[16,48,384]{2,1,0:T(8,128)(2,1)}, bf16[16,48,384]{2,1,0:T(8,128)(2,1)S(1)}, u32[]{:S(2)}, u32[]{:S(2)}) collective-permute-start(bf16[16,48,384]{2,1,0:T(8,128)(2,1)} %get-tuple-element.68), channel_id=1, source_target_pairs={{0,1},{1,0},{2,3},{3,2},{4,5},{5,4},{6,7},{7,6},{8,9},{9,8},{10,11... | collective-permute-start | bytes 1769480 | tf_op jit(solution)/shard_map/ppermute | solution.py:601
  75.0 5.0 %collective-permute-start.3 = (bf16[512,384]{1,0:T(8,128)(2,1)S(1)}, bf16[512,384]{1,0:T(8,128)(2,1)S(1)}, u32[]{:S(2)}, u32[]{:S(2)}) collective-permute-start(bf16[512,384]{1,0:T(8,128)(2,1)S(1)} %get-tuple-element.65), channel_id=1, source_target_pairs={{0,1},{1,0},{2,3},{3,2},{4,5},{5,4},{6,7},{7,6},{8,9},{9,8},{10,11... | collective-permute-start | bytes 1179656 | tf_op jit(solution)/shard_map/ppermute | solution.py:601
  105.8 19.3 %collective-permute-start.17 = (bf16[8,3,48,384]{3,2,1,0:T(8,128)(2,1)S(1)}, bf16[8,3,48,384]{3,2,1,0:T(8,128)(2,1)}, u32[]{:S(2)}, u32[]{:S(2)}) collective-permute-start(bf16[8,3,48,384]{3,2,1,0:T(8,128)(2,1)S(1)} %slice.125), channel_id=1, source_target_pairs={{0,2},{1,5},{2,0},{3,7},{4,6},{5,1},{6,4},{7,3},{8,10},{9,13},{10,... | collective-permute-start | bytes 2654216 | tf_op jit(solution)/shard_map/ppermute | solution.py:597
  109.6 48.7 %collective-permute-start.8 = (bf16[8,192,384]{2,1,0:T(8,128)(2,1)S(1)}, bf16[8,192,384]{2,1,0:T(8,128)(2,1)S(1)}, u32[]{:S(2)}, u32[]{:S(2)}) collective-permute-start(bf16[8,192,384]{2,1,0:T(8,128)(2,1)S(1)} %slice.139), channel_id=1, source_target_pairs={{0,2},{1,5},{2,0},{3,7},{4,6},{5,1},{6,4},{7,3},{8,10},{9,13},{10,... | collective-permute-start | bytes 3538952 | tf_op jit(solution)/shard_map/ppermute | solution.py:597
  122.1 18.6 %collective-permute-start.21 = (bf16[9,48,384]{2,1,0:T(8,128)(2,1)S(1)}, bf16[9,48,384]{2,1,0:T(8,128)(2,1)S(1)}, u32[]{:S(2)}, u32[]{:S(2)}) collective-permute-start(bf16[9,48,384]{2,1,0:T(8,128)(2,1)S(1)} %slice.132), channel_id=1, source_target_pairs={{0,2},{1,5},{2,0},{3,7},{4,6},{5,1},{6,4},{7,3},{8,10},{9,13},{10,... | collective-permute-start | bytes 995336 | tf_op jit(solution)/shard_map/ppermute | solution.py:597
  125.0 35.1 %collective-permute-start.13 = (bf16[8,4,48,384]{3,2,1,0:T(8,128)(2,1)S(1)}, bf16[8,4,48,384]{3,2,1,0:T(8,128)(2,1)S(1)}, u32[]{:S(2)}, u32[]{:S(2)}) collective-permute-start(bf16[8,4,48,384]{3,2,1,0:T(8,128)(2,1)S(1)} %slice.147), channel_id=1, source_target_pairs={{0,2},{1,5},{2,0},{3,7},{4,6},{5,1},{6,4},{7,3},{8,10},{9,13},{10,... | collective-permute-start | bytes 3538952 | tf_op jit(solution)/shard_map/ppermute | solution.py:597
  127.8 28.8 %collective-permute-start.18 = (bf16[4,3,48,384]{3,2,1,0:T(8,128)(2,1)S(1)}, bf16[4,3,48,384]{3,2,1,0:T(8,128)(2,1)S(1)}, u32[]{:S(2)}, u32[]{:S(2)}) collective-permute-start(bf16[4,3,48,384]{3,2,1,0:T(8,128)(2,1)S(1)} %slice.155), channel_id=1, source_target_pairs={{0,4},{1,3},{2,6},{3,1},{4,0},{5,7},{6,2},{7,5},{8,12},{9,11},{10,... | collective-permute-start | bytes 1327112 | tf_op jit(solution)/shard_map/ppermute | solution.py:597
  140.8 7.7 %collective-permute-start.22 = (bf16[5,48,384]{2,1,0:T(8,128)(2,1)S(1)}, bf16[5,48,384]{2,1,0:T(8,128)(2,1)S(1)}, u32[]{:S(2)}, u32[]{:S(2)}) collective-permute-start(bf16[5,48,384]{2,1,0:T(8,128)(2,1)S(1)} %slice.160), channel_id=1, source_target_pairs={{0,4},{1,3},{2,6},{3,1},{4,0},{5,7},{6,2},{7,5},{8,12},{9,11},{10,... | collective-permute-start | bytes 552968 | tf_op jit(solution)/shard_map/ppermute | solution.py:597
  148.5 4.9 %collective-permute-start.23 = (bf16[3,48,384]{2,1,0:T(8,128)(2,1)S(1)}, bf16[3,48,384]{2,1,0:T(8,128)(2,1)S(1)}, u32[]{:S(2)}, u32[]{:S(2)}) collective-permute-start(bf16[3,48,384]{2,1,0:T(8,128)(2,1)S(1)} %slice.161), channel_id=1, source_target_pairs={{0,8},{1,9},{2,10},{3,11},{4,12},{5,13},{6,14},{7,15},{8,0},{9,1},... | collective-permute-start | bytes 331784 | tf_op jit(solution)/shard_map/ppermute | solution.py:597
  153.5 8.8 %collective-permute-start.24 = (bf16[2,48,384]{2,1,0:T(8,128)(2,1)S(1)}, bf16[2,48,384]{2,1,0:T(8,128)(2,1)S(1)}, u32[]{:S(2)}, u32[]{:S(2)}) collective-permute-start(bf16[2,48,384]{2,1,0:T(8,128)(2,1)S(1)} %slice.162), channel_id=1, source_target_pairs={{0,16},{1,17},{2,18},{3,19},{4,20},{5,21},{6,22},{7,23},{8,24},{9,... | collective-permute-start | bytes 221192 | tf_op jit(solution)/shard_map/ppermute | solution.py:597
  156.7 6.8 %collective-permute-start.19 = (bf16[2,3,48,384]{3,2,1,0:T(8,128)(2,1)S(1)}, bf16[2,3,48,384]{3,2,1,0:T(8,128)(2,1)S(1)}, u32[]{:S(2)}, u32[]{:S(2)}) collective-permute-start(bf16[2,3,48,384]{3,2,1,0:T(8,128)(2,1)S(1)} %slice.157), channel_id=1, source_target_pairs={{0,8},{1,9},{2,10},{3,11},{4,12},{5,13},{6,14},{7,15},{8,0},{9,1},... | collective-permute-start | bytes 663560 | tf_op jit(solution)/shard_map/ppermute | solution.py:597
  158.5 9.9 %collective-permute-start.9 = (bf16[4,192,384]{2,1,0:T(8,128)(2,1)S(1)}, bf16[4,192,384]{2,1,0:T(8,128)(2,1)S(1)}, u32[]{:S(2)}, u32[]{:S(2)}) collective-permute-start(bf16[4,192,384]{2,1,0:T(8,128)(2,1)S(1)} %slice.141), channel_id=1, source_target_pairs={{0,4},{1,3},{2,6},{3,1},{4,0},{5,7},{6,2},{7,5},{8,12},{9,11},{10,... | collective-permute-start | bytes 1769480 | tf_op jit(solution)/shard_map/ppermute | solution.py:597
  160.3 14.5 %collective-permute-start.14 = (bf16[4,4,48,384]{3,2,1,0:T(8,128)(2,1)S(1)}, bf16[4,4,48,384]{3,2,1,0:T(8,128)(2,1)S(1)}, u32[]{:S(2)}, u32[]{:S(2)}) collective-permute-start(bf16[4,4,48,384]{3,2,1,0:T(8,128)(2,1)S(1)} %slice.149), channel_id=1, source_target_pairs={{0,4},{1,3},{2,6},{3,1},{4,0},{5,7},{6,2},{7,5},{8,12},{9,11},{10,... | collective-permute-start | bytes 1769480 | tf_op jit(solution)/shard_map/ppermute | solution.py:597
  160.9 41.8 %collective-permute-start.6 = (bf16[512,384]{1,0:T(8,128)(2,1)S(1)}, bf16[512,384]{1,0:T(8,128)(2,1)S(1)}, u32[]{:S(2)}, u32[]{:S(2)}) collective-permute-start(bf16[512,384]{1,0:T(8,128)(2,1)S(1)} %slice_bitcast_fusion.1), channel_id=1, source_target_pairs={{1,0},{3,2},{5,4},{7,6},{9,8},{11,10},{13,12},{15,14},{17,16},{19,... | collective-permute-start | bytes 1179656 | tf_op jit(solution)/shard_map/ppermute | solution.py:773
  162.3 41.9 %collective-permute-start.5 = (bf16[512,768]{1,0:T(8,128)(2,1)S(1)}, bf16[512,768]{1,0:T(8,128)(2,1)S(1)}, u32[]{:S(2)}, u32[]{:S(2)}) collective-permute-start(bf16[512,768]{1,0:T(8,128)(2,1)S(1)} %get-tuple-element.73), channel_id=1, source_target_pairs={{0,1},{1,0},{2,3},{3,2},{4,5},{5,4},{6,7},{7,6},{8,9},{9,8},{10,11... | collective-permute-start | bytes 2359304 | tf_op jit(solution)/shard_map/ppermute | solution.py:601
  163.5 42.6 %collective-permute-start.28 = (bf16[2,48,384]{2,1,0:T(8,128)(2,1)S(1)}, bf16[2,48,384]{2,1,0:T(8,128)(2,1)S(1)}, u32[]{:S(2)}, u32[]{:S(2)}) collective-permute-start(bf16[2,48,384]{2,1,0:T(8,128)(2,1)S(1)} %shard_map.331.refs_3_), channel_id=1, source_target_pairs={{0,1},{1,0},{2,3},{3,2},{4,5},{5,4},{6,7},{7,6},{8,9},{9,8},{10,11... | collective-permute-start | bytes 221192 | tf_op jit(solution)/shard_map/ppermute | solution.py:601
  168.5 7.0 %collective-permute-start.20 = (bf16[1,3,48,384]{3,2,1,0:T(8,128)(2,1)S(1)}, bf16[1,3,48,384]{3,2,1,0:T(8,128)(2,1)S(1)}, u32[]{:S(2)}, u32[]{:S(2)}) collective-permute-start(bf16[1,3,48,384]{3,2,1,0:T(8,128)(2,1)S(1)} %slice.159), channel_id=1, source_target_pairs={{0,16},{1,17},{2,18},{3,19},{4,20},{5,21},{6,22},{7,23},{8,24},{9,... | collective-permute-start | bytes 331784 | tf_op jit(solution)/shard_map/ppermute | solution.py:597
  174.8 9.1 %collective-permute-start.10 = (bf16[2,192,384]{2,1,0:T(8,128)(2,1)S(1)}, bf16[2,192,384]{2,1,0:T(8,128)(2,1)S(1)}, u32[]{:S(2)}, u32[]{:S(2)}) collective-permute-start(bf16[2,192,384]{2,1,0:T(8,128)(2,1)S(1)} %slice.143), channel_id=1, source_target_pairs={{0,8},{1,9},{2,10},{3,11},{4,12},{5,13},{6,14},{7,15},{8,0},{9,1},... | collective-permute-start | bytes 884744 | tf_op jit(solution)/shard_map/ppermute | solution.py:597
  175.5 11.6 %collective-permute-start.15 = (bf16[2,4,48,384]{3,2,1,0:T(8,128)(2,1)S(1)}, bf16[2,4,48,384]{3,2,1,0:T(8,128)(2,1)S(1)}, u32[]{:S(2)}, u32[]{:S(2)}) collective-permute-start(bf16[2,4,48,384]{3,2,1,0:T(8,128)(2,1)S(1)} %slice.151), channel_id=1, source_target_pairs={{0,8},{1,9},{2,10},{3,11},{4,12},{5,13},{6,14},{7,15},{8,0},{9,1},... | collective-permute-start | bytes 884744 | tf_op jit(solution)/shard_map/ppermute | solution.py:597
  183.9 22.2 %collective-permute-start.27 = (bf16[3,48,384]{2,1,0:T(8,128)(2,1)S(1)}, bf16[3,48,384]{2,1,0:T(8,128)(2,1)S(1)}, u32[]{:S(2)}, u32[]{:S(2)}) collective-permute-start(bf16[3,48,384]{2,1,0:T(8,128)(2,1)S(1)} %fusion.3.refs_2_), channel_id=1, source_target_pairs={{0,1},{1,0},{2,3},{3,2},{4,5},{5,4},{6,7},{7,6},{8,9},{9,8},{10,11... | collective-permute-start | bytes 331784 | tf_op jit(solution)/shard_map/ppermute | solution.py:601
  187.1 9.6 %collective-permute-start.11 = (bf16[1,192,384]{2,1,0:T(8,128)(2,1)S(1)}, bf16[1,192,384]{2,1,0:T(8,128)(2,1)S(1)}, u32[]{:S(2)}, u32[]{:S(2)}) collective-permute-start(bf16[1,192,384]{2,1,0:T(8,128)(2,1)S(1)} %slice.145), channel_id=1, source_target_pairs={{0,16},{1,17},{2,18},{3,19},{4,20},{5,21},{6,22},{7,23},{8,24},{9,... | collective-permute-start | bytes 442376 | tf_op jit(solution)/shard_map/ppermute | solution.py:597
  196.7 6.0 %collective-permute-start.16 = (bf16[1,4,48,384]{3,2,1,0:T(8,128)(2,1)S(1)}, bf16[1,4,48,384]{3,2,1,0:T(8,128)(2,1)S(1)}, u32[]{:S(2)}, u32[]{:S(2)}) collective-permute-start(bf16[1,4,48,384]{3,2,1,0:T(8,128)(2,1)S(1)} %slice.153), channel_id=1, source_target_pairs={{0,16},{1,17},{2,18},{3,19},{4,20},{5,21},{6,22},{7,23},{8,24},{9,... | collective-permute-start | bytes 442376 | tf_op jit(solution)/shard_map/ppermute | solution.py:597
  (30 other events, 323.6 us)

commit v2 on v1

v2 whole, which is shorter than its diff:
```python
import functools

import jax
import jax.numpy as jnp
from jax import lax
from jax.experimental import pallas as pl
from jax.experimental.pallas import tpu as pltpu
from jax.sharding import PartitionSpec as P

HEAD = 64
FRESH = 6
PAIR = 2 * HEAD
QB = 256
LOG2E = 1.4426950408889634
GELU_C = 0.7978845608028654
GELU_A = 0.044715
f32 = jnp.float32
bf16 = jnp.bfloat16
NT = (((1,), (1,)), ((), ()))
TN = (((0,), (0,)), ((), ()))
CORE, LENGTH, PLACE, PLACE_OTH, PLACE_Z, PLACE_Z_OTH = 0, 1, 6, 22, 38, 54
V_UP, V_DOWN, V_OUT, V_GAIN2, V_SHIFT2, V_GAIN1, V_SHIFT1, V_QUERY, V_VALUE = 0, 8, 10, 12, 14, 16, 18, 20, 22
V_ROWS = 24


def dot(left, right):
    return jnp.dot(left, right, preferred_element_type=f32)


def dot_nt(left, right):
    return lax.dot_general(left, right, NT, preferred_element_type=f32)


def dot_tn(left, right):
    return lax.dot_general(left, right, TN, preferred_element_type=f32)


def row_of(ref):
    return ref[...].astype(f32).reshape(1, -1)


def normalise(values):
    centre = values - jnp.mean(values, axis=-1, keepdims=True)
    spread = jnp.mean(centre * centre, axis=-1, keepdims=True)
    scale = lax.rsqrt(spread + 1e-05)
    return centre * scale, scale


def params(limit_mb, axes):
    return pltpu.CompilerParams(vmem_limit_bytes=limit_mb << 20, dimension_semantics=("arbitrary",) * axes)


def whole(shape):
    return pl.BlockSpec(shape, lambda *_: (0,) * len(shape))


def cost(micros):
    return pl.CostEstimate(flops=int(micros * 1e8), bytes_accessed=1 << 20, transcendentals=0)


def sds(shape, dtype):
    return jax.ShapeDtypeStruct(shape, dtype)


def project_kernel(scal, own, oth, skip_own, skip_oth, gain, shift, wq, bq, wk, wv, bv, q_ref, k_ref, v_ref, n_ref):
    step = pl.program_id(0)
    core = scal[CORE]
    mine = step < 2
    tokens = jnp.where(mine, own[...], oth[...]).astype(f32)
    xhat, _ = normalise(tokens)
    normed = (xhat * row_of(gain) + row_of(shift)).astype(bf16)
    n_ref[0] = normed
    half = q_ref.shape[2]
    bias = jnp.where(core == 0, row_of(bq)[:, :half], row_of(bq)[:, half:])
    q_ref[0] = (dot(normed, wq[...]) + bias).astype(bf16) * jnp.asarray(HEAD**-0.5, bf16)
    k_ref[0] = dot(normed, wk[...]).astype(bf16)

    @pl.when(core == 0)
    def _():
        v_ref[0] = (dot(normed, wv[...]) + row_of(bv)).astype(bf16)

    @pl.when(core != 0)
    def _():
        v_ref[0] = jnp.where(mine, skip_own[...], skip_oth[...])


def project(scal, own, oth, skip_own, skip_oth, gain, shift, wq, bq, wk, wv, bv):
    rows, width = own.shape
    half = width // 2
    tile = rows // 2
    first = lambda s, sc: (jnp.minimum(s, 1), 0)
    second = lambda s, sc: (jnp.maximum(s - 2, 0), 0)
    col = lambda s, sc: (0, sc[CORE])
    out = lambda s, sc: (s // 2, s % 2, 0)
    return pl.pallas_call(
        project_kernel,
        grid_spec=pltpu.PrefetchScalarGridSpec(
            num_scalar_prefetch=1,
            grid=(4,),
            in_specs=[
                pl.BlockSpec((tile, width), first),
                pl.BlockSpec((tile, width), second),
                pl.BlockSpec((tile, half), first),
                pl.BlockSpec((tile, half), second),
                whole((width,)),
                whole((width,)),
                pl.BlockSpec((width, half), col),
                whole((width,)),
                pl.BlockSpec((width, half), col),
                whole((width, half)),
                whole((half,)),
            ],
            out_specs=[pl.BlockSpec((1, tile, half), out)] * 3 + [pl.BlockSpec((1, tile, width), out)],
        ),
        out_shape=[sds((2, rows, half), bf16)] * 3 + [sds((2, rows, width), bf16)],
        compiler_params=params(56, 1),
    )(scal, own, oth, skip_own, skip_oth, gain, shift, wq, bq, wk, wv, bv)


def first_allowed(scal, total):
    place = lax.broadcasted_iota(jnp.int32, (1, total), 1)
    start = jnp.zeros((1, total), jnp.int32)
    bound = jnp.int32(0)
    for k in range(4):
        bound = bound + scal[LENGTH + k]
        start = jnp.where(place >= bound, bound, start)
    return jnp.where(place >= bound + scal[LENGTH + 4], place, start)


def allowed_block(start, low, high, first_query):
    key = lax.broadcasted_iota(jnp.int32, (high - low, QB), 0) + low
    ok = key >= start
    if high > first_query:
        ok = ok & (key <= lax.broadcasted_iota(jnp.int32, (high - low, QB), 1) + first_query)
    return ok


def head_part(values, h):
    lane = lax.broadcasted_iota(jnp.int32, values.shape, 1)
    return jnp.where((lane < HEAD) if h == 0 else (lane >= HEAD), values, jnp.zeros_like(values))


def key_rows(qb):
    return QB * (qb * (qb + 1) // 2), QB * (qb + 1)


def attend_kernel(scal, q_ref, k_ref, v_ref, o_own, o_oth, p_ref, kb, vt, o_ref):
    core = scal[CORE]
    rows = q_ref.shape[1]
    total = 2 * rows
    for half in range(2):
        rel = core ^ half
        kb[half * rows : (half + 1) * rows, :] = k_ref[rel]
        vt[:, half * rows : (half + 1) * rows] = v_ref[rel].T
    start = first_allowed(scal, total)
    items = [(qb, h) for qb in range(total // QB) for h in range(2)]

    def place(qb):
        return core ^ (qb * QB // rows), pl.ds(qb * QB % rows, QB)

    def scores(qb, h):
        low = qb * QB
        rel, at = place(qb)
        qh = head_part(q_ref[rel, at, :], h)
        return [(a, b, dot_nt(kb[a:b, :], qh)) for a, b in ([(0, low)] if low else []) + [(low, low + QB)]]

    done = {}
    ahead = scores(*items[0])
    for n, (qb, h) in enumerate(items):
        current = ahead
        if n + 1 < len(items):
            ahead = scores(*items[n + 1])
        low = qb * QB
        base, _ = key_rows(qb)
        begin = start[:, low : low + QB]
        peak = None
        masked = []
        for a, b, s in current:
            s = jnp.where(allowed_block(begin, a, b, low), s, -1e30)
            top = jnp.max(s, axis=0, keepdims=True)
            peak = top if peak is None else jnp.maximum(peak, top)
            masked.append((a, b, s))
        peak2 = peak * LOG2E
        raised = [(a, b, jnp.exp2(s * LOG2E - peak2)) for a, b, s in masked]
        summed = None
        for a, b, e in raised:
            part = jnp.sum(e, axis=0, keepdims=True)
            summed = part if summed is None else summed + part
        inverse = 1.0 / summed
        acc = None
        for a, b, e in raised:
            p = (e * inverse).astype(bf16)
            p_ref[0, h, base + a : base + b, :] = p
            part = dot(vt[h * HEAD : (h + 1) * HEAD, a:b], p)
            acc = part if acc is None else acc + part
        done[h] = acc
        if h == 1:
            rel, at = place(qb)
            o_ref[rel, at, :] = jnp.concatenate([done[0], done[1]], axis=0).T.astype(bf16)
    o_own[...] = o_ref[0]
    o_oth[...] = o_ref[1]


def attend(scal, q, k, v):
    _, rows, half = q.shape
    pairs = half // PAIR
    block = pl.BlockSpec((2, rows, PAIR), lambda p, sc: (0, 0, p))
    side = pl.BlockSpec((rows, PAIR), lambda p, sc: (0, p))
    packed = key_rows(2 * rows // QB)[0]
    return pl.pallas_call(
        attend_kernel,
        grid_spec=pltpu.PrefetchScalarGridSpec(
            num_scalar_prefetch=1,
            grid=(pairs,),
            in_specs=[block] * 3,
            out_specs=[side, side, pl.BlockSpec((1, 2, packed, QB), lambda p, sc: (p, 0, 0, 0))],
            scratch_shapes=[
                pltpu.VMEM((2 * rows, PAIR), bf16),
                pltpu.VMEM((PAIR, 2 * rows), bf16),
                pltpu.VMEM((2, rows, PAIR), bf16),
            ],
        ),
        out_shape=[sds((rows, half), bf16)] * 2 + [sds((pairs, 2, packed, QB), bf16)],
        cost_estimate=cost(10),
        compiler_params=params(56, 1),
    )(scal, q, k, v)


def mlp_kernel(
    scal, att_own, att_oth, tok, cot, wo, bo, gain, shift, up, ub, down, db,
    out_ref, gm_ref, ga_keep, ga_send, dn_keep, dn_send, up_keep, up_send, ow_keep, ow_send, vec_ref,
    mid, xhat_ref, scale_ref, normed, normed_t, acc, back, ubias, dtile, sems,
):
    step = pl.program_id(0)
    steps = pl.num_programs(0)
    core = scal[CORE]
    width = tok.shape[1]
    half = width // 2
    chunk = width // 16
    fchunk = half // 2
    parts = width // fchunk
    slot = step & 1

    def att_weight(which):
        return wo[pl.ds(pl.multiple_of(which * half, half), half), :]

    def copies(at, tile):
        found = []
        for n in range(parts):
            for k, (out, side, table) in enumerate(((dn_keep, core, PLACE), (dn_send, 1 - core, PLACE_OTH))):
                cols = pl.ds(pl.multiple_of(side * half, half), half)
                found.append(
                    pltpu.make_async_copy(
                        dtile.at[at, n, :, cols], out.at[scal[table + tile * parts + n]], sems.at[at, n, k]
                    )
                )
        return found

    @pl.when(step == 0)
    def _():
        branch = dot(att_own[...], att_weight(core)) + dot(att_oth[...], att_weight(1 - core)) + row_of(bo)
        middle = tok[...].astype(f32) + branch
        xhat, scale = normalise(middle)
        mid[...] = middle
        xhat_ref[...] = xhat
        scale_ref[...] = scale
        value = (xhat * row_of(gain) + row_of(shift)).astype(bf16)
        normed[...] = value
        normed_t[...] = value.T
        acc[...] = jnp.zeros_like(acc)
        back[...] = jnp.zeros_like(back)
        ubias[...] = row_of(ub)

    tile = (step + (steps // 2) * (1 - core)) & (steps - 1)

    @pl.when(step >= 2)
    def _():
        for copy in copies(slot, tile):
            copy.wait()

    v = dot(normed[...], up[...]) + ubias[:, pl.ds(pl.multiple_of(tile * width, width), width)]
    sq = v * v
    t = jnp.tanh(v * (GELU_C + (GELU_C * GELU_A) * sq))
    half_t = 0.5 * (1.0 + t)
    act = (v * half_t).astype(bf16)
    slope = half_t + (0.5 * v) * (1.0 - t * t) * (GELU_C + (3.0 * GELU_C * GELU_A) * sq)
    acc[...] += dot(act, down[...])
    dtile[slot] = dot_tn(act, cot[...]).astype(bf16).reshape(parts, fchunk, width)
    for copy in copies(slot, tile):
        copy.start()
    grad = (dot_nt(cot[...], down[...]) * slope).astype(bf16)
    back[...] += dot_nt(grad, up[...])
    sums = jnp.sum(grad.astype(f32), axis=0, keepdims=True)
    for g in range(2):
        vec_ref[pl.ds(V_UP + 2 * tile + g, 1), :] = sums[:, g * half : (g + 1) * half]
    dup = dot(normed_t[...], grad).astype(bf16).reshape(16, chunk, width)

    def place_up(ref, table):
        for d in range(16):
            for g in range(2):
                ref[scal[table + d], g] = dup[d, :, g * half : (g + 1) * half]

    pl.when(step < steps // 2)(lambda: place_up(up_send, PLACE_Z_OTH))
    pl.when(step >= steps // 2)(lambda: place_up(up_keep, PLACE_Z))

    @pl.when(step == steps - 1)
    def _():
        out_ref[...] = (mid[...] + acc[...] + row_of(db)).astype(bf16)
        g = back[...]
        xhat = xhat_ref[...]
        grad_out = cot[...].astype(f32)
        weighted = g * row_of(gain)
        dv = scale_ref[...] * (
            weighted
            - jnp.mean(weighted, axis=-1, keepdims=True)
            - xhat * jnp.mean(weighted * xhat, axis=-1, keepdims=True)
        )
        grad_middle = grad_out + dv
        gm_ref[...] = grad_middle
        branch = grad_middle.astype(bf16)

        def put(row, vector):
            vec_ref[row : row + 1, :] = vector[:, :half]
            vec_ref[row + 1 : row + 2, :] = vector[:, half:]

        put(V_DOWN, jnp.sum(grad_out, axis=0, keepdims=True))
        put(V_OUT, jnp.sum(branch.astype(f32), axis=0, keepdims=True))
        put(V_GAIN2, jnp.sum(g * xhat, axis=0, keepdims=True))
        put(V_SHIFT2, jnp.sum(g, axis=0, keepdims=True))
        ga_keep[...] = dot_nt(branch, att_weight(core)).astype(bf16)
        ga_send[...] = dot_nt(branch, att_weight(1 - core)).astype(bf16)
        wide_own = dot_tn(att_own[...], branch).astype(bf16).reshape(8, chunk, width)
        wide_oth = dot_tn(att_oth[...], branch).astype(bf16).reshape(8, chunk, width)

        def spread(keep, send):
            for d in range(8):
                own_place = scal[PLACE + core * 8 + d]
                oth_place = scal[PLACE + (1 - core) * 8 + d]
                ow_keep[own_place] = wide_own[d, :, keep]
                ow_keep[oth_place] = wide_oth[d, :, keep]
                ow_send[scal[PLACE_OTH + core * 8 + d]] = wide_own[d, :, send]
                ow_send[scal[PLACE_OTH + (1 - core) * 8 + d]] = wide_oth[d, :, send]

        left, right = slice(0, half), slice(half, width)
        pl.when(core == 0)(lambda: spread(left, right))
        pl.when(core != 0)(lambda: spread(right, left))
        for at in range(2):
            for copy in copies(at, tile):
                copy.wait()


def mlp(scal, att_own, att_oth, tok, cot, wo, bo, gain, shift, up, ub, down, db):
    rows, width = tok.shape
    half = width // 2
    hidden = up.shape[1]
    steps = hidden // width
    tile = lambda s, sc: (s + (steps // 2) * (1 - sc[CORE])) & (steps - 1)
    share = (16, 2, width // 16, half)
    return pl.pallas_call(
        mlp_kernel,
        grid_spec=pltpu.PrefetchScalarGridSpec(
            num_scalar_prefetch=1,
            grid=(steps,),
            in_specs=[
                whole((rows, half)),
                whole((rows, half)),
                whole((rows, width)),
                whole((rows, width)),
                whole((width, width)),
                whole((width,)),
                whole((width,)),
                whole((width,)),
                pl.BlockSpec((width, width), lambda s, sc: (0, tile(s, sc))),
                whole((hidden,)),
                pl.BlockSpec((width, width), lambda s, sc: (tile(s, sc), 0)),
                whole((width,)),
            ],
            out_specs=[
                whole((rows, width)),
                whole((rows, width)),
                whole((rows, half)),
                whole((rows, half)),
                pl.BlockSpec(memory_space=pl.ANY),
                pl.BlockSpec(memory_space=pl.ANY),
                pl.BlockSpec(share, lambda s, sc: (0, jnp.maximum(s - steps // 2, 0), 0, 0)),
                pl.BlockSpec(share, lambda s, sc: (0, jnp.minimum(s, steps // 2 - 1), 0, 0)),
                whole((16, width // 16, half)),
                whole((16, width // 16, half)),
                whole((16, half)),
            ],
            scratch_shapes=[
                pltpu.VMEM((rows, width), f32),
                pltpu.VMEM((rows, width), f32),
                pltpu.VMEM((rows, 1), f32),
                pltpu.VMEM((rows, width), bf16),
                pltpu.VMEM((width, rows), bf16),
                pltpu.VMEM((rows, width), f32),
                pltpu.VMEM((rows, width), f32),
                pltpu.VMEM((1, hidden), f32),
                pltpu.VMEM((2, 4, half // 2, width), bf16),
                pltpu.SemaphoreType.DMA((2, 4, 2)),
            ],
        ),
        out_shape=[
            sds((rows, width), bf16),
            sds((rows, width), f32),
            sds((rows, half), bf16),
            sds((rows, half), bf16),
            sds((16, half // 2, half), bf16),
            sds((16, half // 2, half), bf16),
            sds((16, steps, width // 16, half), bf16),
            sds((16, steps, width // 16, half), bf16),
            sds((16, width // 16, half), bf16),
            sds((16, width // 16, half), bf16),
            sds((16, half), f32),
        ],
        cost_estimate=cost(28),
        compiler_params=params(44, 1),
    )(scal, att_own, att_oth, tok, cot, wo, bo, gain, shift, up, ub, down, db)


def pair_back(scal, q_ref, k_ref, v_ref, o1, o2, p_ref, do1, do2, n_ref, x, scratch):
    vb, kt, db, ob, dk_acc, dv_acc = scratch
    core = scal[CORE]
    rows = q_ref.shape[1]
    total = 2 * rows
    width = n_ref.shape[2]
    for hf in range(2):
        rel = core ^ hf
        cut = slice(hf * rows, (hf + 1) * rows)
        vb[cut, :] = v_ref[rel]
        kt[:, cut] = k_ref[rel].T
    db[0] = do1[...]
    db[1] = do2[...]
    ob[0] = o1[...]
    ob[1] = o2[...]
    dk_acc[...] = jnp.zeros_like(dk_acc)
    dv_acc[...] = jnp.zeros_like(dv_acc)
    items = [(qb, h) for qb in reversed(range(total // QB)) for h in range(2)]

    def place(qb):
        return core ^ (qb * QB // rows), pl.ds(qb * QB % rows, QB)

    def grad_probs(qb, h):
        rel, at = place(qb)
        return dot_nt(vb[0 : (qb + 1) * QB, :], head_part(db[rel, at, :], h))

    ahead = grad_probs(*items[0])
    parts = []
    for n, (qb, h) in enumerate(items):
        dp = ahead
        if n + 1 < len(items):
            ahead = grad_probs(*items[n + 1])
        rel, at = place(qb)
        base, keys = key_rows(qb)
        cut = slice(h * HEAD, (h + 1) * HEAD)
        if h == 0:
            query_t = q_ref[rel, at, :].T
            grad_t = db[rel, at, :].T
            both = grad_t.astype(f32) * ob[rel, at, :].T.astype(f32)
        delta = jnp.sum(both[cut], axis=0, keepdims=True)
        p = p_ref[0, h, base : base + keys, :]
        ds = (p.astype(f32) * (dp - delta)).astype(bf16)
        dv_acc[cut, 0:keys] += dot_nt(grad_t[cut], p)
        dk_acc[cut, 0:keys] += dot_nt(query_t[cut], ds)
        parts.append(dot(kt[cut, 0:keys], ds))
        if h == 1:
            x[rel, at, 0:PAIR] = (jnp.concatenate(parts, axis=0).T * (HEAD**-0.5)).astype(bf16)
            parts = []
    for hf in range(2):
        rel = core ^ hf
        cut = slice(hf * rows, (hf + 1) * rows)
        x[rel, :, PAIR : 2 * PAIR] = dk_acc[:, cut].T.astype(bf16)
        x[rel, :, 2 * PAIR :] = dv_acc[:, cut].T.astype(bf16)
    grads = x[...].reshape(total, 3 * PAIR)
    dw = dot_tn(n_ref[...].reshape(total, width), grads).astype(bf16).reshape(16, width // 16, 3 * PAIR)
    return dw, jnp.sum(grads.astype(f32), axis=0, keepdims=True)


def first_pair_kernel(scal, *refs):
    inputs, (t_ref, x, sums_ref), scratch = refs[:9], refs[9:12], refs[12:]
    dw, sums = pair_back(scal, *inputs, x, scratch)
    sums_ref[0:1, :] = sums
    for d in range(16):
        t_ref[scal[PLACE + d]] = dw[d]


def second_pair_kernel(scal, *refs):
    inputs, (t_in, ow_keep, ow_recv), (t_ref, x, sums_ref), scratch = refs[:9], refs[9:12], refs[12:15], refs[15:]
    t_ref[:, 0] = t_in[...]
    t_ref[:, 2] = (ow_keep[...].astype(f32) + ow_recv[...].astype(f32)).astype(bf16)
    dw, sums = pair_back(scal, *inputs, x, scratch)
    sums_ref[0:1, :] = sums
    for d in range(16):
        t_ref[scal[PLACE + d], 1] = dw[d]


def last_pair_kernel(scal, *refs):
    inputs, (x0, x1, sums0, sums1, vec_in, own, oth, wq, wk, wv) = refs[:9], refs[9:19]
    (t_ref, gn_ref, gs_ref, dv_own, dv_send), (x, xs, ws, *scratch) = refs[19:24], refs[24:]
    core = scal[CORE]
    dw, sums = pair_back(scal, *inputs, x, scratch)
    for d in range(16):
        t_ref[scal[PLACE + d]] = dw[d]
    rows = own.shape[0]
    half = own.shape[1] // 2
    for p, piece in enumerate((x0, x1, x)):
        left = p * 3 * PAIR
        xs[:, left : left + 3 * PAIR] = piece[...].reshape(2 * rows, 3 * PAIR)
        dv_own[:, p * PAIR : (p + 1) * PAIR] = piece[0, :, 2 * PAIR :]
        dv_send[:, p * PAIR : (p + 1) * PAIR] = piece[1, :, 2 * PAIR :]
        for k, weight in enumerate((wq, wk, wv)):
            ws[:, left + k * PAIR : left + (k + 1) * PAIR] = weight[:, p * PAIR : (p + 1) * PAIR]

    @pl.when(core != 0)
    def _():
        for p in range(3):
            ws[:, p * 3 * PAIR + 2 * PAIR : (p + 1) * 3 * PAIR] = jnp.zeros((ws.shape[0], PAIR), bf16)

    g = dot_nt(xs[...], ws[...])
    gn_ref[...] = g[:rows]
    gs_ref[...] = g[rows:].astype(bf16)
    gains, shifts = 0.0, 0.0
    for rel, tok in ((0, own), (1, oth)):
        xhat, _ = normalise(tok[...].astype(f32))
        part = g[rel * rows : (rel + 1) * rows]
        gains += jnp.sum(part * xhat, axis=0, keepdims=True)
        shifts += jnp.sum(part, axis=0, keepdims=True)
    every = [sums0[0:1, :], sums1[0:1, :], sums]
    query_bias = jnp.concatenate([s[:, :PAIR] for s in every], axis=1)
    value_bias = jnp.concatenate([s[:, 2 * PAIR :] for s in every], axis=1)
    none = jnp.zeros_like(query_bias)
    vec = [vec_in[...], gains[:, :half], gains[:, half:], shifts[:, :half], shifts[:, half:]]
    vec += [jnp.where(core == 0, query_bias, none), jnp.where(core == 0, none, query_bias)]
    vec += [jnp.where(core == 0, value_bias, none), none]
    t_ref[16] = split_high_low(jnp.concatenate(vec, axis=0))


def pair_call(scal, pair, head_args, more):
    rows, width = head_args[8].shape[1:]
    half = width // 2
    chunk = width // 16
    head = pl.BlockSpec((2, rows, PAIR), lambda p, sc: (0, 0, pair))
    rel = pl.BlockSpec((rows, PAIR), lambda p, sc: (0, pair))
    in_specs = [head] * 3 + [
        rel,
        rel,
        pl.BlockSpec((1, 2, key_rows(2 * rows // QB)[0], QB), lambda p, sc: (pair, 0, 0, 0)),
        rel,
        rel,
        whole((2, rows, width)),
    ]
    scratch = [
        pltpu.VMEM((2 * rows, PAIR), bf16),
        pltpu.VMEM((PAIR, 2 * rows), bf16),
        pltpu.VMEM((2, rows, PAIR), bf16),
        pltpu.VMEM((2, rows, PAIR), bf16),
        pltpu.VMEM((PAIR, 2 * rows), f32),
        pltpu.VMEM((PAIR, 2 * rows), f32),
    ]
    grads = sds((2, rows, 3 * PAIR), bf16)
    more_specs = [whole(x.shape) for x in more]
    if pair == 2:
        column = pl.BlockSpec((width, half), lambda p, sc: (0, sc[CORE]))
        more_specs[-3:] = [column, column, whole((width, half))]
        scratch = [
            pltpu.VMEM(grads.shape, bf16),
            pltpu.VMEM((2 * rows, 9 * PAIR), bf16),
            pltpu.VMEM((width, 9 * PAIR), bf16),
        ] + scratch
        out_shape = [
            sds((17, chunk, half), bf16), sds((rows, width), f32), sds((rows, width), bf16), sds((rows, half), bf16),
            sds((rows, half), bf16),
        ]
    else:
        out_shape = [sds((16, 3, chunk, half) if pair else (16, chunk, half), bf16), grads, sds((8, half), f32)]
    return pl.pallas_call(
        (first_pair_kernel, second_pair_kernel, last_pair_kernel)[pair],
        grid_spec=pltpu.PrefetchScalarGridSpec(
            num_scalar_prefetch=1,
            grid=(1,),
            in_specs=in_specs + more_specs,
            out_specs=[whole(x.shape) for x in out_shape],
            scratch_shapes=scratch,
        ),
        out_shape=out_shape,
        cost_estimate=cost(12 if pair == 2 else 8),
        compiler_params=params(44, 1),
    )(scal, *head_args, *more)


def split_high_low(vec):
    high = vec.astype(bf16)
    return jnp.concatenate([high, (vec - high.astype(f32)).astype(bf16)], axis=0)


def join_high_low(block):
    return block[:V_ROWS].astype(f32) + block[V_ROWS:].astype(f32)


def first_norm_back_kernel(scal, tok, gain, gn_own, gn_oth, grad_middle, dv_own, dv_oth, out_ref, skip_ref):
    skip_ref[...] = jnp.where(scal[CORE] == 0, dv_oth[...], dv_own[...])
    xhat, scale = normalise(tok[...].astype(f32))
    weighted = (gn_own[...] + gn_oth[...].astype(f32)) * row_of(gain)
    dv = scale * (
        weighted
        - jnp.mean(weighted, axis=-1, keepdims=True)
        - xhat * jnp.mean(weighted * xhat, axis=-1, keepdims=True)
    )
    out_ref[...] = (grad_middle[...] + dv).astype(bf16)


def first_norm_back(scal, tok, gain, gn_own, gn_oth, grad_middle, dv_own, dv_oth):
    rows, width = tok.shape
    tile = rows // 2
    block = pl.BlockSpec((tile, width), lambda s, sc: (s, 0))
    narrow = pl.BlockSpec((tile, width // 2), lambda s, sc: (s, 0))
    return pl.pallas_call(
        first_norm_back_kernel,
        grid_spec=pltpu.PrefetchScalarGridSpec(
            num_scalar_prefetch=1,
            grid=(2,),
            in_specs=[block, whole((width,)), block, block, block, narrow, narrow],
            out_specs=[block, narrow],
        ),
        out_shape=[sds((rows, width), bf16), sds((rows, width // 2), bf16)],
        cost_estimate=cost(4),
        compiler_params=params(32, 1),
    )(scal, tok, gain, gn_own, gn_oth, grad_middle, dv_own, dv_oth)


def flip(values, bits, dp_count):
    pairs = [((d * 2 + c), ((d ^ bits[c]) * 2 + c)) for d in range(dp_count) for c in range(2)]
    return lax.ppermute(values, ("dp", "seq"), pairs)


def swap(values):
    return lax.ppermute(values, "seq", [(0, 1), (1, 0)])


STAGES = ((1, 2), (2, 1), (4, 4), (8, 8))
STAGES_Z = ((4, 4), (1, 2), (2, 1), (8, 8))


def after(value, *others):
    return lax.optimization_barrier((value,) + others)[0]


class Halving:
    def __init__(self, parts, stages=STAGES):
        self.parts = list(parts)
        self.size = parts[0].shape[0]
        self.stages = stages
        self.stage = 0

    def total(self, low, high):
        out = self.parts[0][low:high]
        for part in self.parts[1:]:
            out = out + part[low:high]
        return out

    def send(self, token):
        *self.parts, token = lax.optimization_barrier((*self.parts, token))
        if self.stage:
            self.parts = [lax.optimization_barrier(self.total(0, self.size))]
        self.size //= 2
        upper = self.total(self.size, 2 * self.size)
        self.parts = self.parts + [flip(upper, self.stages[self.stage], 16)]
        self.stage += 1
        return upper

    def result(self, token=None):
        if token is not None:
            *self.parts, _ = lax.optimization_barrier((*self.parts, token))
        return self.total(0, self.size)


def add_with_vec_kernel(mine, theirs, out):
    count = out.shape[0] - 1
    out[:count] = mine[:count] + theirs[:count]
    out[count] = split_high_low(join_high_low(mine[2 * count]) + join_high_low(theirs[count]))


class HalvingWithVec(Halving):
    def add(self):
        if len(self.parts) > 1:
            mine, theirs = self.parts
            half = theirs.shape[0] - 1
            summed = pl.pallas_call(
                add_with_vec_kernel,
                out_shape=sds(theirs.shape, bf16),
                compiler_params=pltpu.CompilerParams(vmem_limit_bytes=16 << 20),
            )(mine, theirs)
            self.parts = [summed]

    def send(self, token):
        *self.parts, token = lax.optimization_barrier((*self.parts, token))
        self.add()
        buffer = self.parts[0]
        upper = buffer[(buffer.shape[0] - 1) // 2 :]
        self.parts = [buffer, flip(upper, self.stages[self.stage], 16)]
        self.stage += 1
        return upper

    def result(self, token=None):
        self.add()
        return self.parts[0]


def both_sides(core, own, oth, put):
    @pl.when(core == 0)
    def _():
        put(0, own)
        put(1, oth)

    @pl.when(core != 0)
    def _():
        put(1, own)
        put(0, oth)


def finish_feed_kernel(scal, down, up, down2, up2, gu, gd):
    half = down.shape[1]

    def put(side, shares):
        down, up = shares
        gd[:, side * half : (side + 1) * half] = down[...].astype(f32)
        for g in range(up.shape[0]):
            at = (side * up.shape[0] + g) * half
            gu[:, at : at + half] = up[g].astype(f32)

    both_sides(scal[CORE], (down, up), (down2, up2), put)


def finish_heads_kernel(scal, early, late, early2, late2, gq, gk, gv, go, *vectors):
    half = early.shape[2]

    def put(side, shares):
        early, late = shares
        at = side * half
        go[:, at : at + half] = early[2].astype(f32)
        for p, piece in enumerate((early[0], early[1], late[0])):
            cols = slice(at + p * PAIR, at + (p + 1) * PAIR)
            gq[:, cols] = piece[:, :PAIR].astype(f32)
            gk[:, cols] = piece[:, PAIR : 2 * PAIR].astype(f32)
            if side == 0:
                gv[:, p * PAIR : (p + 1) * PAIR] = piece[:, 2 * PAIR :].astype(f32)

    both_sides(scal[CORE], (early, late), (early2, late2), put)
    vec = join_high_low(late[1]) + join_high_low(late2[1])
    for ref, row in zip(vectors, (V_GAIN1, V_SHIFT1, V_QUERY, V_VALUE, V_OUT, V_GAIN2, V_SHIFT2, V_UP, V_DOWN)):
        for k in range(ref.shape[0] // half):
            ref[k * half : (k + 1) * half] = vec[row + k]


def finish(kernel, scal, shares, out_shape):
    out_shape = [sds(shape, f32) for shape in out_shape]
    return pl.pallas_call(
        kernel,
        grid_spec=pltpu.PrefetchScalarGridSpec(
            num_scalar_prefetch=1,
            grid=(1,),
            in_specs=[whole(x.shape) for x in shares],
            out_specs=[whole(s.shape) for s in out_shape],
        ),
        out_shape=out_shape,
        cost_estimate=cost(3),
        compiler_params=params(24, 1),
    )(scal, *shares)


def finish_any(core, down, up, early, late):
    half = down.shape[2]
    vec = lax.psum(join_high_low(late[16]), ("dp", "seq"))

    def columns(pieces):
        mine = jnp.concatenate([x.reshape(-1, x.shape[-1]).astype(f32) for x in pieces], axis=1)
        share = lax.psum_scatter(mine, "dp", scatter_dimension=0, tiled=True)
        other = swap(share)
        return jnp.where(core == 0, jnp.concatenate([share, other], 1), jnp.concatenate([other, share], 1))

    thirds = [early[:, 0], early[:, 1], late[:16]]
    gq, gk, gv = (columns([x[..., i * PAIR : (i + 1) * PAIR] for x in thirds]) for i in range(3))
    go = columns([early[:, 2]])
    gu = columns([up[:, g] for g in range(up.shape[1])])
    gd = columns([down])
    flat = lambda row, n: vec[row : row + n].reshape(-1)
    vectors = [flat(V_GAIN1, 2), flat(V_SHIFT1, 2), flat(V_QUERY, 2), flat(V_VALUE, 1), flat(V_OUT, 2)]
    vectors += [flat(V_GAIN2, 2), flat(V_SHIFT2, 2), flat(V_UP, 8), flat(V_DOWN, 2)]
    return [gq, gk, gv[:, :half], go, gu, gd] + vectors


def per_device(
    dp_count,
    tokens,
    skip_values,
    doc_lengths,
    gain_first,
    shift_first,
    query_weight,
    query_bias,
    key_weight,
    value_weight,
    value_bias,
    out_weight,
    out_bias,
    gain_second,
    shift_second,
    up_weight,
    up_bias,
    down_weight,
    down_bias,
    cotangent,
):
    rows, width = tokens.shape
    hidden = up_weight.shape[1]
    core = lax.axis_index("seq")
    chunks = jnp.arange(16, dtype=jnp.int32)
    if dp_count == 16:
        off = chunks ^ lax.axis_index("dp")
        x_bit, y_bit, z_bits = off & 1, (off >> 1) & 1, ((off >> 2) & 1) * 2 + ((off >> 3) & 1)
        x_first, y_first = x_bit * 8 + y_bit * 4 + z_bits, y_bit * 8 + x_bit * 4 + z_bits
        place, place_oth = jnp.where(core == 0, x_first, y_first), jnp.where(core == 0, y_first, x_first)
        z_first = lambda xy: (xy & 12) // 2 + (xy & 2) * 4 + (xy & 1)
        places = [place, place_oth, z_first(place), z_first(place_oth)]
    else:
        places = [chunks] * 4
    scal = jnp.concatenate([core[None], doc_lengths[0, :5]] + places).astype(jnp.int32)

    tokens_oth = swap(tokens)
    skip_oth = swap(skip_values)
    q, k, v, normed = project(
        scal, tokens, tokens_oth, skip_values, skip_oth, gain_first, shift_first,
        query_weight, query_bias, key_weight, value_weight, value_bias,
    )
    att_own, att_send, probs = attend(scal, q, k, v)
    att_oth = swap(att_send)
    (output, grad_middle, ga_keep, ga_send, dn_keep, dn_send, up_keep, up_send, ow_keep, ow_send, vec) = mlp(
        scal, att_own, att_oth, tokens, cotangent, out_weight, out_bias, gain_second, shift_second,
        up_weight, up_bias, down_weight, down_bias,
    )
    whole_tiles = dp_count == 16
    ga_oth = swap(ga_send)
    dn_send, up_send, ow_send, _ = lax.optimization_barrier((dn_send, up_send, ow_send, ga_oth))
    dn_recv, up_recv, ow_recv = swap(dn_send), swap(up_send), swap(ow_send)
    down = Halving((dn_keep, dn_recv))
    up = Halving((up_keep, up_recv), STAGES_Z)
    head_args = [q, k, v, att_own, att_send, probs, ga_keep, ga_oth, normed]
    t0, x0, sums0 = pair_call(scal, 0, head_args, ())
    token = sums0
    if whole_tiles:
        token = down.send(token)
        token = up.send(token)
    t01, x1, sums1 = pair_call(scal, 1, head_args, (after(t0, token), ow_keep, ow_recv))
    token = sums1
    early = Halving((t01,))
    if whole_tiles:
        token = early.send(token)
        token = down.send(token)
    late, gn_own, gn_send, dv_own, dv_send = pair_call(
        scal, 2, head_args,
        (after(x0, token), x1, sums0, sums1, vec, tokens, tokens_oth, query_weight, key_weight, value_weight),
    )
    gn_oth = swap(gn_send)
    dv_oth = lax.ppermute(dv_send, "seq", [(1, 0)])
    if whole_tiles:
        last = HalvingWithVec((late,))
        token = gn_send
        for chain in (last, down, up, early, last, down):
            token = chain.send(token)
        gn_own, gn_oth, dv_own, dv_oth, token = lax.optimization_barrier((gn_own, gn_oth, dv_own, dv_oth, token))
    grad_tokens, grad_skip = first_norm_back(scal, tokens, gain_first, gn_own, gn_oth, grad_middle, dv_own, dv_oth)
    if whole_tiles:
        token = grad_tokens
        for chain in (up, early, last, up, early, last):
            token = chain.send(token)
        shares = [down.result(token)[0], up.result(token)[0]]
        shares += [swap(x) for x in shares]
        rows_in, wide = width // dp_count, (width // dp_count, width)
        gu, gd = finish(finish_feed_kernel, scal, shares, [(rows_in, hidden), (hidden // dp_count, width)])
        shares = [early.result(token)[0], last.result()]
        shares += [swap(x) for x in shares]
        vectors = [(n,) for n in (width, width, width, width // 2, width, width, width, hidden, width)]
        rest = finish(
            finish_heads_kernel, scal, shares, [wide, wide, (rows_in, width // 2), wide] + vectors
        )
        gq, gk, gv, go, gain1, shift1, gqb, gvb, gob, gain2, shift2, gub, gdb = rest
    else:
        rest = finish_any(core, down.result(), up.result(), early.result(), late)
        gq, gk, gv, go, gu, gd, gain1, shift1, gqb, gvb, gob, gain2, shift2, gub, gdb = rest
    return (
        output, grad_tokens, grad_skip, gain1, shift1, gq, gqb, gk, gv, gvb, go, gob, gain2, shift2, gu, gub, gd, gdb,
    )


def solution(mesh):
    rows, full, shares = P(("dp", "seq"), None), P(), P("dp", None)
    return jax.shard_map(
        functools.partial(per_device, mesh.shape["dp"]),
        mesh=mesh,
        in_specs=(rows, rows, shares) + (full,) * 15 + (rows,),
        out_specs=(
            rows, rows, rows, full, full, shares, full, shares, shares, full, shares, full, full, full, shares, full,
            shares, full,
        ),
        check_vma=False,
    )
```

time: 209 us -> 152 us (0.73)
  waiting for transfers between devices: 66.6 us -> 24.5 us
  Pallas kernels: 96.5 us -> 81.1 us
  starting transfers between devices: 25.4 us -> 33.4 us
  local copies, waits for them, and re-layouts: 12.9 us -> 6.16 us
    ppermute x16, waiting for transfers between devices: 55.4 us -> 18.4 us  [flip(): return lax.ppermute(values, ('dp', 'seq'), pairs)]
    pallas_call x1, Pallas kernels: 43.9 us -> 30.1 us  [mlp(): pl.pallas_call(mlp_kernel, grid_spec=pltpu.PrefetchScalarGridSpec(num_sca...]
    ppermute x16, starting transfers between devices: 20.5 us -> 30.1 us  [flip(): return lax.ppermute(values, ('dp', 'seq'), pairs)]
    unnamed x51 -> x48, local copies, waits for them, and re-layouts: 10.2 us -> 3.52 us
    pallas_call x8 -> x10, Pallas kernels: 35.9 us -> 30.4 us  [the longest x3 24.6 us: pair_call(): pl.pallas_call((first_pair_kernel, second_pair_kernel, last_pair_kernel)[...]
    ppermute x12, waiting for transfers between devices: 11.2 us -> 6.12 us  [swap(): return lax.ppermute(values, 'seq', [(0, 1), (1, 0)])]
    pallas_call x1, Pallas kernels: 5.6 us -> 8.68 us  [project(): pl.pallas_call(project_kernel, grid_spec=pltpu.PrefetchScalarGridSpec(num...]
    add x11 -> x12, other arithmetic: 3.57 us -> 5.45 us  [the longest x11 5.43 us: total(): out = out + part[low:high]]
  transfers between devices with their start and end apart: 29 -> 29, of which waited for: 13 -> 12; matrix products, arithmetic and copies ran while one was open for 4% -> 5% of each run, Pallas kernels for 16% -> 19%
where the time goes in v2:
time: 152 us
  Pallas kernels  81.1 us (53%)
  starting transfers between devices  33.4 us (22%)
  waiting for transfers between devices  24.5 us (16%)
  local copies, waits for them, and re-layouts  6.16 us (4%)
  other arithmetic  5.51 us (4%)
    pallas_call x1, Pallas kernels, mlp(): pl.pallas_call(mlp_kernel, grid_spec=pltpu.PrefetchScalarGridSpec(num_sca...  30.1 us
    ppermute x16, starting transfers between devices, flip(): return lax.ppermute(values, ('dp', 'seq'), pairs)  30.1 us
    pallas_call x3, Pallas kernels, pair_call(): pl.pallas_call((first_pair_kernel, second_pair_kernel, last_pair_kernel)[...  24.6 us
    ppermute x16, waiting for transfers between devices, flip(): return lax.ppermute(values, ('dp', 'seq'), pairs)  18.4 us
    pallas_call x1, Pallas kernels, attend(): pl.pallas_call(attend_kernel, grid_spec=pltpu.PrefetchScalarGridSpec(num_...  12 us
    pallas_call x1, Pallas kernels, project(): pl.pallas_call(project_kernel, grid_spec=pltpu.PrefetchScalarGridSpec(num...  8.68 us
    ppermute x12, waiting for transfers between devices, swap(): return lax.ppermute(values, 'seq', [(0, 1), (1, 0)])  6.12 us
    add x11, other arithmetic, total(): out = out + part[low:high]  5.43 us
  transfers between devices with their start and end apart: 29, of which 12 were waited for; matrix products, arithmetic and copies ran while one was open for 5% of the time, Pallas kernels for 19%

profile of v2, /device:TPU:0, one launch (start us, length us, event | category | flops | bytes accessed | tf_op | source)
XLA Modules:
  0.0 151.9 jit_solution(10071385830774320287)
XLA Ops:
  5.5 8.7 %shard_map.322 = (bf16[2,512,384]{2,1,0:T(8,128)(2,1)}, bf16[2,512,384]{2,1,0:T(8,128)(2,1)}, bf16[2,512,384]{2,1,0:T(8,128)(2,1)}, bf16[2,512,768]{2,1,0:T(8,128)(2,1)}) custom-call(s32[70]{0:T(128)} %concatenate.3.scal, bf16[512,768]{1,0:T(8,128)(2,1)} %tok.3, bf16[512,768]{1,0:T(8,128)(2,1)} %copy-done.8, bf16[512,384]{1,0:T(8,128)(2,1)} %skip_own.1, ...), custom_call_target="tpu_custom_call" | custom-call | tf_op jit(solution)/shard_map/pallas_call | solution.py:95
  14.3 12.0 %shard_map.323 = (bf16[512,384]{1,0:T(8,128)(2,1)}, bf16[512,384]{1,0:T(8,128)(2,1)}, bf16[3,2,2560,256]{3,2,1,0:T(8,128)(2,1)}) custom-call(s32[70]{0:T(128)} %concatenate.3.scal, bf16[2,512,384]{2,1,0:T(8,128)(2,1)} %get-tuple-element.111.q_ref.refs_0_, bf16[2,512,384]{2,1,0:T(8,128)(2,1)} %get-tuple-element.112.k_ref.refs_1_, ...), custom_call_target="tpu_custom_call" | custom-call | flops 1000000000 | bytes 1048576 | tf_op jit(solution)/shard_map/pallas_call | solution.py:210
  26.3 1.9 %collective-permute-done.2.att_oth = bf16[512,384]{1,0:T(8,128)(2,1)S(1)} collective-permute-done((bf16[512,384]{1,0:T(8,128)(2,1)}, bf16[512,384]{1,0:T(8,128)(2,1)S(1)}, u32[]{:S(2)}, u32[]{:S(2)}) %collective-permute-start.2) | collective-permute-done | bytes 393248 | tf_op jit(solution)/shard_map/ppermute | solution.py:638
  29.3 30.1 %shard_map.324 = (bf16[512,768]{1,0:T(8,128)(2,1)}, f32[512,768]{1,0:T(8,128)S(1)}, bf16[512,384]{1,0:T(8,128)(2,1)S(1)}, bf16[512,384]{1,0:T(8,128)(2,1)S(1)}, ...) custom-call(s32[70]{0:T(128)S(1)} %copy-done.14, ...), custom_call_target="tpu_custom_call" | custom-call | flops 2800000000 | bytes 1048576 | tf_op jit(solution)/shard_map/pallas_call | solution.py:359
  59.6 1.6 %collective-permute-done.3.refs_7_ = bf16[512,384]{1,0:T(8,128)(2,1)S(1)} collective-permute-done((bf16[512,384]{1,0:T(8,128)(2,1)S(1)}, bf16[512,384]{1,0:T(8,128)(2,1)S(1)}, u32[]{:S(2)}, u32[]{:S(2)}) %collective-permute-start.3) | collective-permute-done | bytes 393248 | tf_op jit(solution)/shard_map/ppermute | solution.py:638
  61.7 6.3 %shard_map.325 = (bf16[16,48,384]{2,1,0:T(8,128)(2,1)S(1)}, bf16[2,512,384]{2,1,0:T(8,128)(2,1)S(1)}, f32[8,384]{1,0:T(8,128)S(1)}) custom-call(s32[70]{0:T(128)S(1)} %copy-done.14, bf16[2,512,384]{2,1,0:T(8,128)(2,1)S(1)} %copy-done.2, bf16[2,512,384]{2,1,0:T(8,128)(2,1)S(1)} %copy-done.3, bf16[2,512,384]{2,1,0:T(8,128)(2,1)S(1)} %copy-done.4, ...), custom_call_target="tpu_custom_call" | custom-call | flops 800000000 | bytes 1048576 | tf_op jit(solution)/shard_map/pallas_call | solution.py:577
  68.2 2.9 %collective-permute-start.5 = (bf16[8,192,384]{2,1,0:T(8,128)(2,1)S(1)}, bf16[8,192,384]{2,1,0:T(8,128)(2,1)}, u32[]{:S(2)}, u32[]{:S(2)}) collective-permute-start(bf16[8,192,384]{2,1,0:T(8,128)(2,1)S(1)} %slice_add_fusion.1), channel_id=1, source_target_pairs={{0,2},{1,5},{2,0},{3,7},{4,6},{5,1},{6,4},{7,3},{8,10},{9,13},{10,... | collective-permute-start | bytes 3538952 | tf_op jit(solution)/shard_map/ppermute | solution.py:634
  72.6 1.6 %collective-permute-start.14 = (bf16[8,4,48,384]{3,2,1,0:T(8,128)(2,1)S(1)}, bf16[8,4,48,384]{3,2,1,0:T(8,128)(2,1)}, u32[]{:S(2)}, u32[]{:S(2)}) collective-permute-start(bf16[8,4,48,384]{3,2,1,0:T(8,128)(2,1)S(1)} %slice_add_fusion), channel_id=1, source_target_pairs={{0,8},{1,9},{2,10},{3,11},{4,12},{5,13},{6,14},{7,15},{8,0},{9,1},... | collective-permute-start | bytes 3538952 | tf_op jit(solution)/shard_map/ppermute | solution.py:634
  74.2 6.6 %shard_map.326 = (bf16[16,3,48,384]{3,2,1,0:T(8,128)(2,1)S(1)}, bf16[2,512,384]{2,1,0:T(8,128)(2,1)S(1)}, f32[8,384]{1,0:T(8,128)S(1)}) custom-call(s32[70]{0:T(128)S(1)} %copy-done.14, bf16[2,512,384]{2,1,0:T(8,128)(2,1)S(1)} %copy-done.2, bf16[2,512,384]{2,1,0:T(8,128)(2,1)S(1)} %copy-done.3, bf16[2,512,384]{2,1,0:T(8,128)(2,1)S(1)} %copy-done.4, ...), custom_call_target="tpu_custom_call" | custom-call | flops 800000000 | bytes 1048576 | tf_op jit(solution)/shard_map/pallas_call | solution.py:577
  81.9 3.5 %collective-permute-done.5 = bf16[8,192,384]{2,1,0:T(8,128)(2,1)} collective-permute-done((bf16[8,192,384]{2,1,0:T(8,128)(2,1)S(1)}, bf16[8,192,384]{2,1,0:T(8,128)(2,1)}, u32[]{:S(2)}, u32[]{:S(2)}) %collective-permute-start.5) | collective-permute-done | bytes 1179680 | tf_op jit(solution)/shard_map/ppermute | solution.py:634
  87.0 2.1 %collective-permute-start.10 = (bf16[4,192,384]{2,1,0:T(8,128)(2,1)S(1)}, bf16[4,192,384]{2,1,0:T(8,128)(2,1)S(1)}, u32[]{:S(2)}, u32[]{:S(2)}) collective-permute-start(bf16[4,192,384]{2,1,0:T(8,128)(2,1)S(1)} %slice.132), channel_id=1, source_target_pairs={{0,4},{1,3},{2,6},{3,1},{4,0},{5,7},{6,2},{7,5},{8,12},{9,11},{10,... | collective-permute-start | bytes 1769480 | tf_op jit(solution)/shard_map/ppermute | solution.py:634
  90.7 11.7 %shard_map.327 = (bf16[17,48,384]{2,1,0:T(8,128)(2,1)S(1)}, f32[512,768]{1,0:T(8,128)}, bf16[512,768]{1,0:T(8,128)(2,1)S(1)}, bf16[512,384]{1,0:T(8,128)(2,1)S(1)}, bf16[512,384]{1,0:T(8,128)(2,1)S(1)}) custom-call(s32[70]{0:T(128)S(1)} %copy-done.14, bf16[2,512,384]{2,1,0:T(8,128)(2,1)S(1)} %copy-done.2, bf16[2,512,384]{2,1,0:T(8,128)(2,1)S(1)} %copy-done.3, ...), custom_call_target="tpu_custom_call" | custom-call | flops 1200000000 | bytes 1048576 | tf_op jit(solution)/shard_map/pallas_call | solution.py:577
  104.0 1.8 %add_add_fusion = bf16[8,4,48,384]{3,2,1,0:T(8,128)(2,1)S(1)} fusion(bf16[8,4,48,384]{3,2,1,0:T(8,128)(2,1)} %collective-permute-done.14, bf16[16,4,48,384]{3,2,1,0:T(8,128)(2,1)} %collective-permute-done.6, bf16[16,4,48,384]{3,2,1,0:T(8,128)(2,1)S(1)} %copy-done.22), kind=kLoop, calls=%fused_computation | loop fusion | flops 1179648 | bytes 4718592 | tf_op jit(solution)/shard_map/add | solution.py:659
  112.2 3.4 %collective-permute-done.11 = bf16[2,192,384]{2,1,0:T(8,128)(2,1)S(1)} collective-permute-done((bf16[2,192,384]{2,1,0:T(8,128)(2,1)S(1)}, bf16[2,192,384]{2,1,0:T(8,128)(2,1)S(1)}, u32[]{:S(2)}, u32[]{:S(2)}) %collective-permute-start.11) | collective-permute-done | bytes 294944 | tf_op jit(solution)/shard_map/ppermute | solution.py:634
  115.7 2.5 %shard_map.329 = (bf16[512,768]{1,0:T(8,128)(2,1)}, bf16[512,384]{1,0:T(8,128)(2,1)}) custom-call(s32[70]{0:T(128)S(1)} %copy-done.14, bf16[512,768]{1,0:T(8,128)(2,1)S(1)} %copy-done.1, bf16[768]{0:T(1024)(128)(2,1)S(1)} %copy-done.15, f32[512,768]{1,0:T(8,128)S(1)} %copy-done.11, bf16[512,768]{1,0:T(8,128)(2,1)S(1)} %collective-permute-done.8.gn_oth, ...), custom_call_target="tpu_custom_call" | custom-call | flops 400000000 | bytes 1048576 | tf_op jit(solution)/shard_map/pallas_call | solution.py:618
  118.3 1.6 %collective-permute-start.18 = (bf16[2,4,48,384]{3,2,1,0:T(8,128)(2,1)S(1)}, bf16[2,4,48,384]{3,2,1,0:T(8,128)(2,1)S(1)}, u32[]{:S(2)}, u32[]{:S(2)}) collective-permute-start(bf16[2,4,48,384]{3,2,1,0:T(8,128)(2,1)S(1)} %slice.138), channel_id=1, source_target_pairs={{0,4},{1,3},{2,6},{3,1},{4,0},{5,7},{6,2},{7,5},{8,12},{9,11},{10,... | collective-permute-start | bytes 884744 | tf_op jit(solution)/shard_map/ppermute | solution.py:634
  120.4 2.6 %collective-permute-start.25 = (bf16[1,192,384]{2,1,0:T(8,128)(2,1)S(1)}, bf16[1,192,384]{2,1,0:T(8,128)(2,1)S(1)}, u32[]{:S(2)}, u32[]{:S(2)}) collective-permute-start(bf16[1,192,384]{2,1,0:T(8,128)(2,1)S(1)} %slice.137), channel_id=1, source_target_pairs={{0,16},{1,17},{2,18},{3,19},{4,20},{5,21},{6,22},{7,23},{8,24},{9,... | collective-permute-start | bytes 442376 | tf_op jit(solution)/shard_map/ppermute | solution.py:634
  123.1 2.0 %collective-permute-start.17 = (bf16[2,3,48,384]{3,2,1,0:T(8,128)(2,1)S(1)}, bf16[2,3,48,384]{3,2,1,0:T(8,128)(2,1)S(1)}, u32[]{:S(2)}, u32[]{:S(2)}) collective-permute-start(bf16[2,3,48,384]{3,2,1,0:T(8,128)(2,1)S(1)} %slice.139), channel_id=1, source_target_pairs={{0,8},{1,9},{2,10},{3,11},{4,12},{5,13},{6,14},{7,15},{8,0},{9,1},... | collective-permute-start | bytes 663560 | tf_op jit(solution)/shard_map/ppermute | solution.py:634
  125.1 2.0 %collective-permute-done.19.theirs = bf16[5,48,384]{2,1,0:T(8,128)(2,1)S(1)} collective-permute-done((bf16[5,48,384]{2,1,0:T(8,128)(2,1)S(1)}, bf16[5,48,384]{2,1,0:T(8,128)(2,1)S(1)}, u32[]{:S(2)}, u32[]{:S(2)}) %collective-permute-start.19) | collective-permute-done | bytes 184352 | tf_op jit(solution)/shard_map/ppermute | solution.py:634
  127.2 2.0 %collective-permute-start.21 = (bf16[3,48,384]{2,1,0:T(8,128)(2,1)S(1)}, bf16[3,48,384]{2,1,0:T(8,128)(2,1)S(1)}, u32[]{:S(2)}, u32[]{:S(2)}) collective-permute-start(bf16[3,48,384]{2,1,0:T(8,128)(2,1)S(1)} %slice.140), channel_id=1, source_target_pairs={{0,8},{1,9},{2,10},{3,11},{4,12},{5,13},{6,14},{7,15},{8,0},{9,1},... | collective-permute-start | bytes 331784 | tf_op jit(solution)/shard_map/ppermute | solution.py:634
  129.2 2.7 %collective-permute-start.26 = (bf16[1,4,48,384]{3,2,1,0:T(8,128)(2,1)S(1)}, bf16[1,4,48,384]{3,2,1,0:T(8,128)(2,1)S(1)}, u32[]{:S(2)}, u32[]{:S(2)}) collective-permute-start(bf16[1,4,48,384]{3,2,1,0:T(8,128)(2,1)S(1)} %slice.141), channel_id=1, source_target_pairs={{0,16},{1,17},{2,18},{3,19},{4,20},{5,21},{6,22},{7,23},{8,24},{9,... | collective-permute-start | bytes 442376 | tf_op jit(solution)/shard_map/ppermute | solution.py:634
  132.6 4.4 %collective-permute-start.20 = (bf16[1,3,48,384]{3,2,1,0:T(8,128)(2,1)S(1)}, bf16[1,3,48,384]{3,2,1,0:T(8,128)(2,1)S(1)}, u32[]{:S(2)}, u32[]{:S(2)}) collective-permute-start(bf16[1,3,48,384]{3,2,1,0:T(8,128)(2,1)S(1)} %slice.142), channel_id=1, source_target_pairs={{0,16},{1,17},{2,18},{3,19},{4,20},{5,21},{6,22},{7,23},{8,24},{9,... | collective-permute-start | bytes 331784 | tf_op jit(solution)/shard_map/ppermute | solution.py:634
  139.3 6.9 %collective-permute-done.20 = bf16[1,3,48,384]{3,2,1,0:T(8,128)(2,1)S(1)} collective-permute-done((bf16[1,3,48,384]{3,2,1,0:T(8,128)(2,1)S(1)}, bf16[1,3,48,384]{3,2,1,0:T(8,128)(2,1)S(1)}, u32[]{:S(2)}, u32[]{:S(2)}) %collective-permute-start.20) | collective-permute-done | bytes 110624 | tf_op jit(solution)/shard_map/ppermute | solution.py:634
  150.2 1.6 %shard_map.334 = (f32[48,3072]{1,0:T(8,128)}, f32[192,768]{1,0:T(8,128)}) custom-call(s32[70]{0:T(128)S(1)} %copy-done.14, bf16[192,384]{1,0:T(8,128)(2,1)S(1)} %add_bitcast_fusion.1.down, bf16[4,48,384]{2,1,0:T(8,128)(2,1)S(1)} %add_bitcast_fusion.up, bf16[192,384]{1,0:T(8,128)(2,1)S(1)} %collective-permute-done.27.down2, ...), custom_call_target="tpu_custom_call" | custom-call | flops 300000000 | bytes 1048576 | tf_op jit(solution)/shard_map/pallas_call | solution.py:758
  (126 shorter events, 28.2 us)
Async XLA Ops:
  0.7 3.2 %collective-permute-start = (bf16[512,768]{1,0:T(8,128)(2,1)}, bf16[512,768]{1,0:T(8,128)(2,1)S(1)}, u32[]{:S(2)}, u32[]{:S(2)}) collective-permute-start(bf16[512,768]{1,0:T(8,128)(2,1)} %tok.3), channel_id=1, source_target_pairs={{0,1},{1,0},{2,3},{3,2},{4,5},{5,4},{6,7},{7,6},{8,9},{9,8},{10,11... | collective-permute-start | bytes 2359304 | tf_op jit(solution)/shard_map/ppermute | solution.py:638
  61.2 6.9 %collective-permute-start.4 = (bf16[16,192,384]{2,1,0:T(8,128)(2,1)}, bf16[16,192,384]{2,1,0:T(8,128)(2,1)S(1)}, u32[]{:S(2)}, u32[]{:S(2)}) collective-permute-start(bf16[16,192,384]{2,1,0:T(8,128)(2,1)} %get-tuple-element.126), channel_id=1, source_target_pairs={{0,1},{1,0},{2,3},{3,2},{4,5},{5,4},{6,7},{7,6},{8,9},{9,8},{10,11... | collective-permute-start | bytes 7077896 | tf_op jit(solution)/shard_map/ppermute | solution.py:638
  61.3 9.8 %collective-permute-start.6 = (bf16[16,4,48,384]{3,2,1,0:T(8,128)(2,1)}, bf16[16,4,48,384]{3,2,1,0:T(8,128)(2,1)}, u32[]{:S(2)}, u32[]{:S(2)}) collective-permute-start(bf16[16,4,48,384]{3,2,1,0:T(8,128)(2,1)} %get-tuple-element.132), channel_id=1, source_target_pairs={{0,1},{1,0},{2,3},{3,2},{4,5},{5,4},{6,7},{7,6},{8,9},{9,8},{10,11... | collective-permute-start | bytes 7077896 | tf_op jit(solution)/shard_map/ppermute | solution.py:638
  68.2 17.2 %collective-permute-start.5 = (bf16[8,192,384]{2,1,0:T(8,128)(2,1)S(1)}, bf16[8,192,384]{2,1,0:T(8,128)(2,1)}, u32[]{:S(2)}, u32[]{:S(2)}) collective-permute-start(bf16[8,192,384]{2,1,0:T(8,128)(2,1)S(1)} %slice_add_fusion.1), channel_id=1, source_target_pairs={{0,2},{1,5},{2,0},{3,7},{4,6},{5,1},{6,4},{7,3},{8,10},{9,13},{10,... | collective-permute-start | bytes 3538952 | tf_op jit(solution)/shard_map/ppermute | solution.py:634
  71.1 3.1 %collective-permute-start.7 = (bf16[16,48,384]{2,1,0:T(8,128)(2,1)S(1)}, bf16[16,48,384]{2,1,0:T(8,128)(2,1)S(1)}, u32[]{:S(2)}, u32[]{:S(2)}) collective-permute-start(bf16[16,48,384]{2,1,0:T(8,128)(2,1)S(1)} %get-tuple-element.137), channel_id=1, source_target_pairs={{0,1},{1,0},{2,3},{3,2},{4,5},{5,4},{6,7},{7,6},{8,9},{9,8},{10,11... | collective-permute-start | bytes 1769480 | tf_op jit(solution)/shard_map/ppermute | solution.py:638
  72.6 30.6 %collective-permute-start.14 = (bf16[8,4,48,384]{3,2,1,0:T(8,128)(2,1)S(1)}, bf16[8,4,48,384]{3,2,1,0:T(8,128)(2,1)}, u32[]{:S(2)}, u32[]{:S(2)}) collective-permute-start(bf16[8,4,48,384]{3,2,1,0:T(8,128)(2,1)S(1)} %slice_add_fusion), channel_id=1, source_target_pairs={{0,8},{1,9},{2,10},{3,11},{4,12},{5,13},{6,14},{7,15},{8,0},{9,1},... | collective-permute-start | bytes 3538952 | tf_op jit(solution)/shard_map/ppermute | solution.py:634
  87.0 16.1 %collective-permute-start.10 = (bf16[4,192,384]{2,1,0:T(8,128)(2,1)S(1)}, bf16[4,192,384]{2,1,0:T(8,128)(2,1)S(1)}, u32[]{:S(2)}, u32[]{:S(2)}) collective-permute-start(bf16[4,192,384]{2,1,0:T(8,128)(2,1)S(1)} %slice.132), channel_id=1, source_target_pairs={{0,4},{1,3},{2,6},{3,1},{4,0},{5,7},{6,2},{7,5},{8,12},{9,11},{10,... | collective-permute-start | bytes 1769480 | tf_op jit(solution)/shard_map/ppermute | solution.py:634
  89.2 19.9 %collective-permute-start.13 = (bf16[8,3,48,384]{3,2,1,0:T(8,128)(2,1)}, bf16[8,3,48,384]{3,2,1,0:T(8,128)(2,1)S(1)}, u32[]{:S(2)}, u32[]{:S(2)}) collective-permute-start(bf16[8,3,48,384]{3,2,1,0:T(8,128)(2,1)} %slice.104), channel_id=1, source_target_pairs={{0,2},{1,5},{2,0},{3,7},{4,6},{5,1},{6,4},{7,3},{8,10},{9,13},{10,... | collective-permute-start | bytes 2654216 | tf_op jit(solution)/shard_map/ppermute | solution.py:634
  102.4 13.3 %collective-permute-start.8 = (bf16[512,768]{1,0:T(8,128)(2,1)S(1)}, bf16[512,768]{1,0:T(8,128)(2,1)S(1)}, u32[]{:S(2)}, u32[]{:S(2)}) collective-permute-start(bf16[512,768]{1,0:T(8,128)(2,1)S(1)} %get-tuple-element.148), channel_id=1, source_target_pairs={{0,1},{1,0},{2,3},{3,2},{4,5},{5,4},{6,7},{7,6},{8,9},{9,8},{10,11... | collective-permute-start | bytes 2359304 | tf_op jit(solution)/shard_map/ppermute | solution.py:638
  102.4 8.1 %collective-permute-start.12 = (bf16[9,48,384]{2,1,0:T(8,128)(2,1)S(1)}, bf16[9,48,384]{2,1,0:T(8,128)(2,1)S(1)}, u32[]{:S(2)}, u32[]{:S(2)}) collective-permute-start(bf16[9,48,384]{2,1,0:T(8,128)(2,1)S(1)} %slice.108), channel_id=1, source_target_pairs={{0,2},{1,5},{2,0},{3,7},{4,6},{5,1},{6,4},{7,3},{8,10},{9,13},{10,... | collective-permute-start | bytes 995336 | tf_op jit(solution)/shard_map/ppermute | solution.py:634
  105.9 12.3 %collective-permute-start.16 = (bf16[4,4,48,384]{3,2,1,0:T(8,128)(2,1)S(1)}, bf16[4,4,48,384]{3,2,1,0:T(8,128)(2,1)S(1)}, u32[]{:S(2)}, u32[]{:S(2)}) collective-permute-start(bf16[4,4,48,384]{3,2,1,0:T(8,128)(2,1)S(1)} %slice.134), channel_id=1, source_target_pairs={{0,2},{1,5},{2,0},{3,7},{4,6},{5,1},{6,4},{7,3},{8,10},{9,13},{10,... | collective-permute-start | bytes 1769480 | tf_op jit(solution)/shard_map/ppermute | solution.py:634
  107.5 8.2 %collective-permute-start.11 = (bf16[2,192,384]{2,1,0:T(8,128)(2,1)S(1)}, bf16[2,192,384]{2,1,0:T(8,128)(2,1)S(1)}, u32[]{:S(2)}, u32[]{:S(2)}) collective-permute-start(bf16[2,192,384]{2,1,0:T(8,128)(2,1)S(1)} %slice.133), channel_id=1, source_target_pairs={{0,8},{1,9},{2,10},{3,11},{4,12},{5,13},{6,14},{7,15},{8,0},{9,1},... | collective-permute-start | bytes 884744 | tf_op jit(solution)/shard_map/ppermute | solution.py:634
  109.0 6.7 %collective-permute-start.9 = (bf16[512,384]{1,0:T(8,128)(2,1)S(1)}, bf16[512,384]{1,0:T(8,128)(2,1)S(1)}, u32[]{:S(2)}, u32[]{:S(2)}) collective-permute-start(bf16[512,384]{1,0:T(8,128)(2,1)S(1)} %get-tuple-element.150), channel_id=1, source_target_pairs={{1,0},{3,2},{5,4},{7,6},{9,8},{11,10},{13,12},{15,14},{17,16},{19,... | collective-permute-start | bytes 1179656 | tf_op jit(solution)/shard_map/ppermute | solution.py:865
  110.5 12.5 %collective-permute-start.15 = (bf16[4,3,48,384]{3,2,1,0:T(8,128)(2,1)S(1)}, bf16[4,3,48,384]{3,2,1,0:T(8,128)(2,1)S(1)}, u32[]{:S(2)}, u32[]{:S(2)}) collective-permute-start(bf16[4,3,48,384]{3,2,1,0:T(8,128)(2,1)S(1)} %slice.135), channel_id=1, source_target_pairs={{0,4},{1,3},{2,6},{3,1},{4,0},{5,7},{6,2},{7,5},{8,12},{9,11},{10,... | collective-permute-start | bytes 1327112 | tf_op jit(solution)/shard_map/ppermute | solution.py:634
  118.3 10.8 %collective-permute-start.18 = (bf16[2,4,48,384]{3,2,1,0:T(8,128)(2,1)S(1)}, bf16[2,4,48,384]{3,2,1,0:T(8,128)(2,1)S(1)}, u32[]{:S(2)}, u32[]{:S(2)}) collective-permute-start(bf16[2,4,48,384]{3,2,1,0:T(8,128)(2,1)S(1)} %slice.138), channel_id=1, source_target_pairs={{0,4},{1,3},{2,6},{3,1},{4,0},{5,7},{6,2},{7,5},{8,12},{9,11},{10,... | collective-permute-start | bytes 884744 | tf_op jit(solution)/shard_map/ppermute | solution.py:634
  119.9 7.2 %collective-permute-start.19 = (bf16[5,48,384]{2,1,0:T(8,128)(2,1)S(1)}, bf16[5,48,384]{2,1,0:T(8,128)(2,1)S(1)}, u32[]{:S(2)}, u32[]{:S(2)}) collective-permute-start(bf16[5,48,384]{2,1,0:T(8,128)(2,1)S(1)} %slice.136), channel_id=1, source_target_pairs={{0,4},{1,3},{2,6},{3,1},{4,0},{5,7},{6,2},{7,5},{8,12},{9,11},{10,... | collective-permute-start | bytes 552968 | tf_op jit(solution)/shard_map/ppermute | solution.py:634
  120.4 18.8 %collective-permute-start.25 = (bf16[1,192,384]{2,1,0:T(8,128)(2,1)S(1)}, bf16[1,192,384]{2,1,0:T(8,128)(2,1)S(1)}, u32[]{:S(2)}, u32[]{:S(2)}) collective-permute-start(bf16[1,192,384]{2,1,0:T(8,128)(2,1)S(1)} %slice.137), channel_id=1, source_target_pairs={{0,16},{1,17},{2,18},{3,19},{4,20},{5,21},{6,22},{7,23},{8,24},{9,... | collective-permute-start | bytes 442376 | tf_op jit(solution)/shard_map/ppermute | solution.py:634
  123.1 9.4 %collective-permute-start.17 = (bf16[2,3,48,384]{3,2,1,0:T(8,128)(2,1)S(1)}, bf16[2,3,48,384]{3,2,1,0:T(8,128)(2,1)S(1)}, u32[]{:S(2)}, u32[]{:S(2)}) collective-permute-start(bf16[2,3,48,384]{3,2,1,0:T(8,128)(2,1)S(1)} %slice.139), channel_id=1, source_target_pairs={{0,8},{1,9},{2,10},{3,11},{4,12},{5,13},{6,14},{7,15},{8,0},{9,1},... | collective-permute-start | bytes 663560 | tf_op jit(solution)/shard_map/ppermute | solution.py:634
  127.2 11.0 %collective-permute-start.21 = (bf16[3,48,384]{2,1,0:T(8,128)(2,1)S(1)}, bf16[3,48,384]{2,1,0:T(8,128)(2,1)S(1)}, u32[]{:S(2)}, u32[]{:S(2)}) collective-permute-start(bf16[3,48,384]{2,1,0:T(8,128)(2,1)S(1)} %slice.140), channel_id=1, source_target_pairs={{0,8},{1,9},{2,10},{3,11},{4,12},{5,13},{6,14},{7,15},{8,0},{9,1},... | collective-permute-start | bytes 331784 | tf_op jit(solution)/shard_map/ppermute | solution.py:634
  129.2 17.0 %collective-permute-start.26 = (bf16[1,4,48,384]{3,2,1,0:T(8,128)(2,1)S(1)}, bf16[1,4,48,384]{3,2,1,0:T(8,128)(2,1)S(1)}, u32[]{:S(2)}, u32[]{:S(2)}) collective-permute-start(bf16[1,4,48,384]{3,2,1,0:T(8,128)(2,1)S(1)} %slice.141), channel_id=1, source_target_pairs={{0,16},{1,17},{2,18},{3,19},{4,20},{5,21},{6,22},{7,23},{8,24},{9,... | collective-permute-start | bytes 442376 | tf_op jit(solution)/shard_map/ppermute | solution.py:634
  132.6 13.6 %collective-permute-start.20 = (bf16[1,3,48,384]{3,2,1,0:T(8,128)(2,1)S(1)}, bf16[1,3,48,384]{3,2,1,0:T(8,128)(2,1)S(1)}, u32[]{:S(2)}, u32[]{:S(2)}) collective-permute-start(bf16[1,3,48,384]{3,2,1,0:T(8,128)(2,1)S(1)} %slice.142), channel_id=1, source_target_pairs={{0,16},{1,17},{2,18},{3,19},{4,20},{5,21},{6,22},{7,23},{8,24},{9,... | collective-permute-start | bytes 331784 | tf_op jit(solution)/shard_map/ppermute | solution.py:634
  138.2 9.2 %collective-permute-start.22 = (bf16[2,48,384]{2,1,0:T(8,128)(2,1)S(1)}, bf16[2,48,384]{2,1,0:T(8,128)(2,1)S(1)}, u32[]{:S(2)}, u32[]{:S(2)}) collective-permute-start(bf16[2,48,384]{2,1,0:T(8,128)(2,1)S(1)} %slice.143), channel_id=1, source_target_pairs={{0,16},{1,17},{2,18},{3,19},{4,20},{5,21},{6,22},{7,23},{8,24},{9,... | collective-permute-start | bytes 221192 | tf_op jit(solution)/shard_map/ppermute | solution.py:634
  139.2 11.0 %collective-permute-start.27 = (bf16[192,384]{1,0:T(8,128)(2,1)S(1)}, bf16[192,384]{1,0:T(8,128)(2,1)S(1)}, u32[]{:S(2)}, u32[]{:S(2)}) collective-permute-start(bf16[192,384]{1,0:T(8,128)(2,1)S(1)} %add_bitcast_fusion.1.down), channel_id=1, source_target_pairs={{0,1},{1,0},{2,3},{3,2},{4,5},{5,4},{6,7},{7,6},{8,9},{9,8},{10,11... | collective-permute-start | bytes 442376 | tf_op jit(solution)/shard_map/ppermute | solution.py:638
  146.2 4.0 %collective-permute-start.28 = (bf16[4,48,384]{2,1,0:T(8,128)(2,1)S(1)}, bf16[4,48,384]{2,1,0:T(8,128)(2,1)S(1)}, u32[]{:S(2)}, u32[]{:S(2)}) collective-permute-start(bf16[4,48,384]{2,1,0:T(8,128)(2,1)S(1)} %add_bitcast_fusion.up), channel_id=1, source_target_pairs={{0,1},{1,0},{2,3},{3,2},{4,5},{5,4},{6,7},{7,6},{8,9},{9,8},{10,11... | collective-permute-start | bytes 442376 | tf_op jit(solution)/shard_map/ppermute | solution.py:638
  (29 other events, 329.0 us)
